TPU v7x, 256 devices: a whole 4x4x8 slice. The times are simulated.
256 devices in a mesh: dp: 8 (over y, x_lo), seq: 32 (over x_hi, z, core).
Axes of the slice: x: 4 (x_hi: 2, x_lo: 2; x = x_hi * 2 + x_lo), y: 4, z: 8, core: 2. Of those that a mesh axis runs over, the one named last changes fastest.
Arguments:
- inputs: bfloat16 [8, 16384, 768], P('dp', 'seq'), may hold values from -6 to 6
- cotangent: bfloat16 [8, 16384, 768], P('dp', 'seq'), may hold values from -6 to 6
- gain_first: float32 [768], replicated, may hold values from 0.5 to 1.5
- gain_second: float32 [768], replicated, may hold values from 0.5 to 1.5
- value_w: bfloat16 [192, 768], replicated, may hold values from -0.4375 to 0.4375
- gate_w: bfloat16 [192, 768], replicated, may hold values from -0.4375 to 0.4375
- out_w: bfloat16 [192, 768], replicated, may hold values from -0.4375 to 0.4375
- up_w: bfloat16 [192, 3072], replicated, may hold values from -0.4375 to 0.4375
- down_w: bfloat16 [768, 768], replicated, may hold values from -0.21875 to 0.21875
- first_blocks: bfloat16 [64, 256, 256], P('seq'), may hold values from -0.375 to 0.375
- second_blocks: bfloat16 [256, 64, 64], P('seq'), may hold values from -0.75 to 0.75
Outputs:
- layer_out: bfloat16 [8, 16384, 768], P('dp', 'seq')
- grad_input: bfloat16 [8, 16384, 768], P('dp', 'seq')
- grad_value_w: float32 [192, 768], P(None, ('dp', 'seq'))
- grad_gate_w: float32 [192, 768], P(None, ('dp', 'seq'))
- grad_out_w: float32 [192, 768], P(None, ('dp', 'seq'))
- grad_up_w: float32 [192, 3072], P(None, ('dp', 'seq'))
- grad_down_w: float32 [768, 768], P(None, ('dp', 'seq'))
- grad_gain_first: float32 [768], P(('dp', 'seq'))
- grad_gain_second: float32 [768], P(('dp', 'seq'))
- grad_first_blocks: float32 [64, 256, 256], P('seq')
- grad_second_blocks: float32 [256, 64, 64], P('seq')
All inputs are finite; a program needn't handle non-finite values.
Results may differ from a plain program's by a relative error of at most 0.025.
Values may be sent and summed in bfloat16 or wider, within the bound.
A program may use at most 128 MiB of HBM per device.

v0:
```python
import math

import jax
import jax.numpy as jnp
from jax import lax
from jax.sharding import PartitionSpec as P

NBLK = 4
BLOCK = 256


EPS = 1e-06


def gelu_exact(values):
    return jax.nn.gelu(values, approximate=False)


def normalize(rows_in, gain_vec):
    factor = lax.rsqrt(jnp.mean(rows_in * rows_in, axis=-1, keepdims=True) + EPS)
    unit_rows = rows_in * factor
    return (unit_rows, factor, (unit_rows * gain_vec).astype(jnp.bfloat16))


def norm_back(grad_in, unit_rows, factor, gain_vec):
    scaled = grad_in * gain_vec
    back_rows = factor * (scaled - unit_rows * jnp.mean(scaled * unit_rows, axis=-1, keepdims=True))
    return (back_rows, jnp.sum(grad_in * unit_rows, axis=0))


def blocked(act_in, weight):
    row_count = act_in.shape[0]
    width_in = weight.shape[0]
    wide_w = weight.reshape(width_in, NBLK, -1)
    split = act_in.reshape(row_count, NBLK, width_in)
    return jnp.einsum("rnd,dne->rne", split, wide_w, preferred_element_type=jnp.float32).reshape(
        row_count, -1
    )


def blocked_back(grads, weight):
    row_count = grads.shape[0]
    width_in = weight.shape[0]
    wide_w = weight.reshape(width_in, NBLK, -1)
    split = grads.reshape(row_count, NBLK, -1)
    return jnp.einsum("rne,dne->rnd", split, wide_w, preferred_element_type=jnp.float32).reshape(
        row_count, -1
    )


def blocked_grad(act_in, grads):
    row_count = act_in.shape[0]
    left = act_in.reshape(row_count, NBLK, -1)
    right = grads.reshape(row_count, NBLK, -1)
    return jnp.einsum("rnd,rne->dne", left, right, preferred_element_type=jnp.float32).reshape(
        left.shape[2], -1
    )


def to_columns(grid_rows, step_fn):
    return step_fn(lax.all_to_all(grid_rows, "seq", split_axis=2, concat_axis=1, tiled=True))


def to_rows(grid_cols):
    return lax.all_to_all(grid_cols, "seq", split_axis=1, concat_axis=2, tiled=True)


def body(
    inputs,
    cotangent,
    gain_first,
    gain_second,
    value_w,
    gate_w,
    out_w,
    up_w,
    down_w,
    first_blocks,
    second_blocks,
):
    log_count, tok_rows, dmodel = inputs.shape
    row_count = log_count * tok_rows
    a_blocks = first_blocks.shape[0]
    total_logs = log_count * lax.axis_size("dp")
    row_scale = 1.0 / math.sqrt(total_logs * tok_rows * lax.axis_size("seq"))
    mix_scale = 1.0 / math.sqrt(total_logs * dmodel)
    rows_in = inputs.reshape(row_count, dmodel).astype(jnp.float32)
    unit_first, factor_first, normed_first = normalize(rows_in, gain_first)
    value_rows = blocked(normed_first, value_w).astype(jnp.bfloat16)
    gate_rows = blocked(normed_first, gate_w).astype(jnp.bfloat16)
    value_grid = value_rows.reshape(log_count, a_blocks, BLOCK, dmodel)
    first_mix = jnp.einsum(
        "abk,lakc->labc", first_blocks, value_grid, preferred_element_type=jnp.float32
    ).astype(jnp.bfloat16)

    def second_step(column_piece):
        mixed_cols = jnp.einsum(
            "bij,ljbc->libc", second_blocks, column_piece, preferred_element_type=jnp.float32
        ).astype(jnp.bfloat16)
        return (to_rows(mixed_cols), column_piece)

    mixed_grid, first_cols = to_columns(first_mix, second_step)
    mixed_rows = mixed_grid.reshape(row_count, dmodel)
    y_rows = (gate_rows.astype(jnp.float32) * mixed_rows.astype(jnp.float32)).astype(jnp.bfloat16)
    mid_rows = (rows_in + blocked(y_rows, out_w)).astype(jnp.bfloat16)
    mid_f = mid_rows.astype(jnp.float32)
    unit_second, factor_second, normed_second = normalize(mid_f, gain_second)
    hidden_pre = blocked(normed_second, up_w)
    act_f, gelu_back = jax.vjp(gelu_exact, hidden_pre)
    act_rows = act_f.astype(jnp.bfloat16)
    layer_out = (
        (mid_f + blocked(act_rows, down_w))
        .astype(jnp.bfloat16)
        .reshape(log_count, tok_rows, dmodel)
    )
    grad_rows = cotangent.reshape(row_count, dmodel)
    d_act = blocked_back(grad_rows, down_w)
    d_pre = gelu_back(d_act)[0].astype(jnp.bfloat16)
    grad_down = blocked_grad(act_rows, grad_rows) * row_scale
    grad_up = blocked_grad(normed_second, d_pre) * row_scale
    d_second = blocked_back(d_pre, up_w)
    d_mid_norm, gain_two = norm_back(d_second, unit_second, factor_second, gain_second)
    d_mid = (grad_rows.astype(jnp.float32) + d_mid_norm).astype(jnp.bfloat16)
    grad_out = blocked_grad(y_rows, d_mid) * row_scale
    d_y = blocked_back(d_mid, out_w)
    d_gate = (d_y * mixed_rows.astype(jnp.float32)).astype(jnp.bfloat16)
    d_mixed = (d_y * gate_rows.astype(jnp.float32)).astype(jnp.bfloat16)

    def second_back(column_piece):
        back_cols = jnp.einsum(
            "bij,libc->ljbc", second_blocks, column_piece, preferred_element_type=jnp.float32
        ).astype(jnp.bfloat16)
        return (to_rows(back_cols), column_piece)

    d_first, d_mixed_cols = to_columns(
        d_mixed.reshape(log_count, a_blocks, BLOCK, dmodel), second_back
    )
    grad_second = (
        jnp.einsum("libc,ljbc->bij", d_mixed_cols, first_cols, preferred_element_type=jnp.float32)
        * mix_scale
    )
    grad_first = (
        jnp.einsum("labc,lakc->abk", d_first, value_grid, preferred_element_type=jnp.float32)
        * mix_scale
    )
    d_value = (
        jnp.einsum("abk,labc->lakc", first_blocks, d_first, preferred_element_type=jnp.float32)
        .astype(jnp.bfloat16)
        .reshape(row_count, dmodel)
    )
    grad_value = blocked_grad(normed_first, d_value) * row_scale
    grad_gate = blocked_grad(normed_first, d_gate) * row_scale
    d_first_norm = blocked_back(d_value, value_w) + blocked_back(d_gate, gate_w)
    d_in_norm, gain_one = norm_back(d_first_norm, unit_first, factor_first, gain_first)
    grad_input = (
        (d_mid.astype(jnp.float32) + d_in_norm)
        .astype(jnp.bfloat16)
        .reshape(log_count, tok_rows, dmodel)
    )
    grad_first, grad_second = (
        lax.psum(grad_first.astype(jnp.bfloat16), "dp").astype(jnp.float32),
        lax.psum(grad_second.astype(jnp.bfloat16), "dp").astype(jnp.float32),
    )
    gain_one = (gain_one * row_scale).reshape(1, dmodel)
    gain_two = (gain_two * row_scale).reshape(1, dmodel)
    shards = (
        lax.psum_scatter(grad_value, ("dp", "seq"), scatter_dimension=1, tiled=True),
        lax.psum_scatter(grad_gate, ("dp", "seq"), scatter_dimension=1, tiled=True),
        lax.psum_scatter(grad_out, ("dp", "seq"), scatter_dimension=1, tiled=True),
        lax.psum_scatter(grad_up, ("dp", "seq"), scatter_dimension=1, tiled=True),
        lax.psum_scatter(grad_down, ("dp", "seq"), scatter_dimension=1, tiled=True),
        lax.psum_scatter(gain_one, ("dp", "seq"), scatter_dimension=1, tiled=True),
        lax.psum_scatter(gain_two, ("dp", "seq"), scatter_dimension=1, tiled=True),
    )
    return (
        layer_out,
        grad_input,
        shards[0],
        shards[1],
        shards[2],
        shards[3],
        shards[4],
        shards[5].reshape(-1),
        shards[6].reshape(-1),
        grad_first,
        grad_second,
    )


def solution(mesh):
    in_specs = (
        P("dp", "seq", None),
        P("dp", "seq", None),
        P(),
        P(),
        P(),
        P(),
        P(),
        P(),
        P(),
        P("seq", None, None),
        P("seq", None, None),
    )
    out_specs = (
        P("dp", "seq", None),
        P("dp", "seq", None),
        P(None, ("dp", "seq")),
        P(None, ("dp", "seq")),
        P(None, ("dp", "seq")),
        P(None, ("dp", "seq")),
        P(None, ("dp", "seq")),
        P(("dp", "seq")),
        P(("dp", "seq")),
        P("seq", None, None),
        P("seq", None, None),
    )
    return jax.shard_map(body, mesh=mesh, in_specs=in_specs, out_specs=out_specs, check_vma=False)
```

profile of v0, /device:TPU:1, one launch (start us, length us, event | category | flops | bytes accessed | tf_op | source)
XLA Modules:
  0.0 571.8 jit_solution(11749983020433287225)
XLA Ops:
  7.2 1.5 copy.112
  9.7 1.4 fusion.51
  11.1 2.9 convert_element_type.221
  14.0 3.0 copy.145
  17.0 1.6 fusion.47
  18.6 1.8 copy.116
  20.4 35.3 %all_to_all.54 = bf16[1,2,256,768]{3,1,0,2:T(2,128)(2,1)S(1)} all-to-all(bf16[1,2,256,768]{3,1,0,2:T(2,128)(2,1)} %copy.116), channel_id=1, replica_groups=mesh['dp'=8,'seq'=32] {'seq'}, dimensions={2} | all-to-all | bytes 1572864 | tf_op jit(solution)/shard_map/all_to_all | solution.py:61
  55.8 1.7 copy.118
  57.5 2.3 reshape.425
  60.1 1.3 copy.119
  61.4 6.5 %all-to-all-start.1 = ((bf16[1,64,8,768]{3,2,0,1:T(8,128)(2,1)}), bf16[1,64,8,768]{3,2,0,1:T(8,128)(2,1)}, u32[]{:S(2)}, u32[]{:S(2)}) async-start(bf16[1,64,8,768]{3,2,0,1:T(8,128)(2,1)} %copy.119), calls=%async_computation.1 | async-start | bytes 1572864 | tf_op jit(solution)/shard_map/all_to_all | solution.py:65
  68.0 1.3 reshape.423
  69.3 2.2 reshape.426
  71.7 2.3 copy.127
  74.0 2.4 copy.125
  76.4 1.4 convolution_convert_fusion.1
  77.8 13.2 %all-to-all-done.1 = bf16[1,64,8,768]{3,2,0,1:T(8,128)(2,1)} async-done(((bf16[1,64,8,768]{3,2,0,1:T(8,128)(2,1)}), bf16[1,64,8,768]{3,2,0,1:T(8,128)(2,1)}, u32[]{:S(2)}, u32[]{:S(2)}) %all-to-all-start.1) | async-done | bytes 786464 | tf_op jit(solution)/shard_map/all_to_all | solution.py:65
  90.9 1.2 copy_bitcast_fusion
  92.2 2.9 reshape.437
  95.1 1.9 copy.121
  97.0 3.0 fusion.39
  100.0 15.4 %fusion.9 = (bf16[512,4,768]{2,0,1:T(8,128)(2,1)}, f32[512,4,768]{2,0,1:T(8,128)S(1)}, f32[4,512,768]{2,1,0:T(8,128)S(1)}) fusion(bf16[24,4,8,768]{3,2,1,0:T(8,128)(2,1)S(1)} %bitcast.264, bf16[512,4,192]{0,2,1:T(8,128)(2,1)S(1)} %get-tuple-element.60, f32[4,192]{1,0:T(4,128)S(1)} %mul.319, f32[512]{0:T(512)S(1)} %add_rsqrt_fusion), kind=kOutput, calls=%fused_computation.17 | convolution fusion | flops 707788800 | bytes 17699840 | tf_op jit(solution)/shard_map/rnd,dne->rne/dot_general | solution.py:36
  115.4 3.0 fusion.6
  118.4 1.9 fusion.38
  120.8 1.2 copy-done.5
  122.1 1.5 fusion.44
  123.6 3.2 convert_element_type.247
  126.8 3.7 copy.132
  130.4 28.7 %all_to_all.55 = bf16[1,2,256,768]{3,1,0,2:T(2,128)(2,1)S(1)} all-to-all(bf16[1,2,256,768]{3,1,0,2:T(2,128)(2,1)} %copy.132), channel_id=1, replica_groups=mesh['dp'=8,'seq'=32] {'seq'}, dimensions={2} | all-to-all | bytes 1572864 | tf_op jit(solution)/shard_map/all_to_all | solution.py:61
  159.2 1.7 copy.134
  161.0 3.0 reshape.432
  163.9 1.5 fusion.48
  165.5 1.3 copy.136
  166.8 6.5 %all-to-all-start.3 = ((bf16[1,64,8,768]{3,2,0,1:T(8,128)(2,1)}), bf16[1,64,8,768]{3,2,0,1:T(8,128)(2,1)}, u32[]{:S(2)}, u32[]{:S(2)}) async-start(bf16[1,64,8,768]{3,2,0,1:T(8,128)(2,1)} %copy.136), calls=%async_computation.3 | async-start | bytes 1572864 | tf_op jit(solution)/shard_map/all_to_all | solution.py:65
  173.3 3.0 multiply_bitcast_fusion
  176.3 1.7 copy.155
  178.1 1.3 convolution_multiply_fusion.2
  179.4 1.3 convolution_multiply_fusion.1
  180.8 0.8 copy-done.1
  181.8 2.2 convolution_multiply_fusion
  184.0 1.0 fusion.57
  185.0 11.2 %all-to-all-done.3 = bf16[1,64,8,768]{3,2,0,1:T(8,128)(2,1)} async-done(((bf16[1,64,8,768]{3,2,0,1:T(8,128)(2,1)}), bf16[1,64,8,768]{3,2,0,1:T(8,128)(2,1)}, u32[]{:S(2)}, u32[]{:S(2)}) %all-to-all-start.3) | async-done | bytes 786464 | tf_op jit(solution)/shard_map/all_to_all | solution.py:65
  196.2 2.2 fusion.52
  198.5 1.6 fusion.49
  200.2 1.7 copy.139
  201.9 2.4 reshape_reshape.9
  204.3 1.3 convolution_multiply_fusion.3
  206.4 3.0 copy.130
  209.5 4.6 fusion.81
  214.0 3.0 copy.126
  217.1 3.1 copy.123
  220.2 1.4 fusion.69
  221.6 1.8 fusion.40
  223.5 3.2 copy.143
  226.7 76.6 %all-reduce.7 = (f32[1,768]{1,0:T(1,128)S(1)}, f32[1,768]{1,0:T(1,128)S(1)}) all-reduce(f32[1,768]{1,0:T(1,128)S(1)} %mul.375, f32[1,768]{1,0:T(1,128)S(1)} %mul.378), channel_id=7, replica_groups=mesh['dp'=8,'seq'=32] {'dp','seq'}, use_global_device_ids=true, to_apply=%region_10.0.clone | all-reduce | flops 1536 | bytes 12288
  304.0 4.6 add_convert_fusion
  308.6 1.8 convert_element_type.257
  310.4 1.6 convert_element_type.259
  312.0 247.2 %all-reduce.13.cloned.1.call-done = (f32[192,768]{0,1:T(8,128)}, f32[192,768]{0,1:T(8,128)}, f32[192,768]{0,1:T(8,128)}, f32[192,3072]{1,0:T(8,128)}, f32[768,768]{0,1:T(8,128)}) async-done(((f32[192,768]{0,1:T(8,128)}, f32[192,768]{0,1:T(8,128)}, f32[192,768]{0,1:T(8,128)}, f32[192,3072]{1,0:T(8,128)}, f32[768,768]{0,1:T(8,128)}), (f32[192,768]{0,1:T(8,128)}, f32[192,768]{0,1:T(8,128)}, ...) | async-done | bytes 6488080
  559.2 1.0 constant_dynamic-slice_fusion.3
  560.2 0.7 copy.146
  560.9 1.4 constant_dynamic-slice_fusion.2
  562.3 1.3 constant_dynamic-slice_fusion.6
  563.7 1.3 constant_dynamic-slice_fusion.4
  (99 shorter events, 4.0 us)
Async XLA Ops:
  7.2 9.8 %copy-start = (bf16[2,256,256]{2,1,0:T(8,128)(2,1)S(1)}, bf16[2,256,256]{2,1,0:T(8,128)(2,1)}, u32[]{:S(2)}) copy-start(bf16[2,256,256]{2,1,0:T(8,128)(2,1)} %param.20) | copy-start | bytes 786436
  7.2 1.6 copy-start.11
  7.2 1.8 copy-start.33
  7.2 1.9 copy-start.30
  9.4 4.5 copy-start.26
  9.7 66.7 %copy-start.2 = (bf16[512,4,192]{0,2,1:T(8,128)(2,1)}, bf16[512,4,192]{0,2,1:T(8,128)(2,1)S(1)}, u32[]{:S(2)}) copy-start(bf16[512,4,192]{0,2,1:T(8,128)(2,1)S(1)} %multiply_convert_fusion) | copy-start | bytes 2359300
  55.7 4.0 copy-start.29
  59.8 1.7 copy-start.15
  60.1 11.5 %copy-start.35 = (f32[768]{0:T(1024)S(1)}, f32[768]{0:T(1024)}, u32[]{:S(2)}) copy-start(f32[768]{0:T(1024)} %param.14) | copy-start | bytes 9220
  61.4 29.5 %all-to-all-start.1 = ((bf16[1,64,8,768]{3,2,0,1:T(8,128)(2,1)}), bf16[1,64,8,768]{3,2,0,1:T(8,128)(2,1)}, u32[]{:S(2)}, u32[]{:S(2)}) async-start(bf16[1,64,8,768]{3,2,0,1:T(8,128)(2,1)} %copy.119), calls=%async_computation.1 | async-start | bytes 1572864 | tf_op jit(solution)/shard_map/all_to_all | solution.py:65
  69.3 8.4 %copy-start.24 = (bf16[192,4,192]{2,1,0:T(4,128)(2,1)}, bf16[192,4,192]{2,1,0:T(4,128)(2,1)S(1)}, u32[]{:S(2)}) copy-start(bf16[192,4,192]{2,1,0:T(4,128)(2,1)S(1)} %reshape.423) | copy-start | bytes 884740
  97.0 3.0 copy-start.38
  100.0 20.3 %copy-start.9 = (bf16[512,4,192]{0,2,1:T(8,128)(2,1)}, bf16[512,4,192]{0,2,1:T(8,128)(2,1)S(1)}, u32[]{:S(2)}) copy-start(bf16[512,4,192]{0,2,1:T(8,128)(2,1)S(1)} %get-tuple-element.60) | copy-start | bytes 2359300
  100.0 15.4 %copy-start.7 = (bf16[1,512,768]{1,2,0:T(8,128)(2,1)S(1)}, bf16[1,512,768]{1,2,0:T(8,128)(2,1)}, u32[]{:S(2)}) copy-start(bf16[1,512,768]{1,2,0:T(8,128)(2,1)} %copy.127) | copy-start | bytes 2359300
  100.0 15.4 %copy-start.22 = (bf16[768,768]{0,1:T(8,128)(2,1)S(1)}, bf16[768,768]{0,1:T(8,128)(2,1)}, u32[]{:S(2)}) copy-start(bf16[768,768]{0,1:T(8,128)(2,1)} %copy.125) | copy-start | bytes 3538948
  118.4 1.9 copy-start.10
  120.3 3.3 copy-start.21
  120.3 1.7 copy-start.5
  120.3 1.8 copy-start.23
  120.3 3.3 copy-start.31
  122.1 1.6 copy-start.18
  166.8 29.4 %all-to-all-start.3 = ((bf16[1,64,8,768]{3,2,0,1:T(8,128)(2,1)}), bf16[1,64,8,768]{3,2,0,1:T(8,128)(2,1)}, u32[]{:S(2)}, u32[]{:S(2)}) async-start(bf16[1,64,8,768]{3,2,0,1:T(8,128)(2,1)} %copy.136), calls=%async_computation.3 | async-start | bytes 1572864 | tf_op jit(solution)/shard_map/all_to_all | solution.py:65
  173.3 135.3 %all-reduce.15.cloned.1.call-start = ((), (), s32[]{:S(2)}) async-start(), calls=%async_computation.5 | async-start | bytes 786432 | tf_op jit(solution)/shard_map/psum | solution.py:161
  176.3 1.7 copy-start.3
  176.3 1.8 copy-start.13
  178.0 1.3 copy-start.6
  178.0 1.4 copy-start.19
  179.4 2.2 copy-start.1
  179.4 2.4 copy-start.8
  181.8 2.2 copy-start.16
  181.8 2.2 copy-start.17
  181.8 14.4 %copy-start.28 = (bf16[2,256,768]{2,1,0:T(8,128)(2,1)S(1)}, bf16[2,256,768]{2,1,0:T(8,128)(2,1)}, u32[]{:S(2)}) copy-start(bf16[2,256,768]{2,1,0:T(8,128)(2,1)} %copy.145) | copy-start | bytes 2359300
  198.5 5.9 %copy-start.4 = (bf16[512,4,192]{0,2,1:T(8,128)(2,1)S(1)}, bf16[512,4,192]{0,2,1:T(8,128)(2,1)}, u32[]{:S(2)}) copy-start(bf16[512,4,192]{0,2,1:T(8,128)(2,1)} %copy-done.2) | copy-start | bytes 2359300
  198.5 360.7 %all-reduce.13.cloned.1.call-start = ((), (), s32[]{:S(2)}) async-start(), calls=%async_computation.4 | async-start | bytes 14155776
  205.7 0.7 copy-start.37
  217.1 4.5 copy-start.14
  220.2 1.4 copy-start.25
  223.4 80.5 %copy-start.12 = (bf16[1,512,768]{2,1,0:T(8,128)(2,1)S(1)}, bf16[1,512,768]{2,1,0:T(8,128)(2,1)}, u32[]{:S(2)}) copy-start(bf16[1,512,768]{2,1,0:T(8,128)(2,1)} %param.11) | copy-start | bytes 2359300
  223.4 80.5 %copy-start.20 = (f32[1,512,768]{2,1,0:T(8,128)S(1)}, f32[1,512,768]{2,1,0:T(8,128)}, u32[]{:S(2)}) copy-start(f32[1,512,768]{2,1,0:T(8,128)} %copy.130) | copy-start | bytes 4718596
  223.4 80.5 %copy-start.27 = (bf16[1,512,768]{2,1,0:T(8,128)(2,1)S(1)}, bf16[1,512,768]{2,1,0:T(8,128)(2,1)}, u32[]{:S(2)}) copy-start(bf16[1,512,768]{2,1,0:T(8,128)(2,1)} %param.12) | copy-start | bytes 2359300
  223.4 80.6 %copy-start.32 = (f32[512]{0:T(512)S(1)}, f32[512]{0:T(512)}, u32[]{:S(2)}) copy-start(f32[512]{0:T(512)} %copy-done.31) | copy-start | bytes 6148
  223.4 80.6 %copy-start.34 = (f32[768]{0:T(1024)S(1)}, f32[768]{0:T(1024)}, u32[]{:S(2)}) copy-start(f32[768]{0:T(1024)} %param.13) | copy-start | bytes 9220
  223.4 80.6 %copy-start.36 = (f32[768]{0:T(1024)S(1)}, f32[768]{0:T(1024)}, u32[]{:S(2)}) copy-start(f32[768]{0:T(1024)} %param.14) | copy-start | bytes 9220
Sparse Core Ops, SparseCore 0:
  198.6 71.6 all-reduce.14
  277.9 281.2 all-reduce.12
where the time goes:
time: 574 us; the launch traced here: 572 us
  waiting for transfers between devices  272 us (47%)
  blocking collectives  141 us (25%)
  local copies, waits for them, and re-layouts  69 us (12%)
  matrix products  52.8 us (9%)
  between operations  14.5 us (3%)
  starting transfers between devices  13.1 us (2%)
  other arithmetic  10.2 us (2%)
    unnamed x3, waiting for transfers between devices  247 us
    unnamed x1, blocking collectives  76.6 us
    all_to_all x2, blocking collectives, to_columns(): lax.all_to_all(grid_rows, 'seq', split_axis=2, concat_axis=1, tiled=True)  64 us
    dot_general x5, matrix products, blocked(): jnp.einsum('rnd,dne->rne', split, wide_w, preferred_element_type=jnp.floa...  25.8 us
    all_to_all x2, waiting for transfers between devices, to_rows(): lax.all_to_all(grid_cols, 'seq', split_axis=1, concat_axis=2, tiled=True)  24.4 us
    unnamed x85, local copies, waits for them, and re-layouts  13.7 us
    all_to_all x2, starting transfers between devices, to_rows(): lax.all_to_all(grid_cols, 'seq', split_axis=1, concat_axis=2, tiled=True)  13 us
  transfers between devices with their start and end apart: 4, of which 3 were waited for; matrix products, arithmetic and copies ran while one was open for 10% of the time, Pallas kernels for 0%

commit v1 on v0

v1 whole, which is shorter than its diff:
```python
import functools
import math

import jax
import jax.numpy as jnp
import numpy as np
from jax import lax
from jax.experimental import pallas as pl
from jax.experimental.pallas import tpu as pltpu
from jax.sharding import PartitionSpec as P

MESH = pl.DeviceIdType.MESH
F32 = jnp.float32
BF16 = jnp.bfloat16
EPS = 1e-6
NY, NXL, NXH, NZ, NC = 4, 2, 2, 8, 2
NS, ND = NXH * NZ * NC, NY * NXL
D, NB, DB, HB, ROWS, HALF = 768, 4, 192, 768, 512, 256
ROW_SCALE = 1.0 / math.sqrt(131072.0)
MIX_SCALE = 1.0 / math.sqrt(6144.0)
EW, LW = 2048, 256
GL, UL = 1152, 1280
VMEM_LIMIT = 60 * 2**20


def dot(a, b, ca=1, cb=0):
    return lax.dot_general(a, b, (((ca,), (cb,)), ((), ())), preferred_element_type=F32)


def constants():
    one = lambda shape, pairs: _onehot(shape, pairs)
    row, col = [], []
    for ii in range(2):
        for d in range(NS):
            for bl in range(8):
                row.append(ii * 256 + d * 8 + bl)
                col.append(bl * 64 + 2 * d + ii)
    perm_m = one((512, 512), (row, col))
    expand = one((64, 512), (np.arange(512) // 8, np.arange(512)))
    out = np.arange(192)
    c, rem = out // 96, out % 96
    perm3 = one((192, 192), (out, rem // 3 * 6 + c * 3 + rem % 3))
    perm12 = one((192, 192), (out, rem // 12 * 24 + c * 12 + rem % 12))
    dest, t = np.arange(48) // 3, np.arange(48) % 3
    fold = np.concatenate([one((256, 48), (dest * 16 + 3 * f + t, np.arange(48))) for f in range(3)], axis=1)
    z, t = np.arange(96) // 12, np.arange(96) % 12
    low, high = t < 6, t >= 6
    ufold = np.concatenate(
        [
            one((128, 96), ((z * 16 + 9 + t)[low], np.arange(96)[low])),
            one((128, 96), ((z * 16 + 3 + t)[high], np.arange(96)[high])),
        ],
        axis=1,
    )
    return perm_m, expand, perm3, perm12, fold, ufold


def _onehot(shape, pairs):
    array = np.zeros(shape, np.float32)
    array[pairs[0], pairs[1]] = 1.0
    return array


def remote(src, dst, ssem, rsem, device):
    return pltpu.make_async_remote_copy(
        src_ref=src, dst_ref=dst, send_sem=ssem, recv_sem=rsem, device_id=device, device_id_type=MESH
    )


def seq_peer(k, me):
    g, t = k // 8, k % 8
    dx, dc = 1 - g // 2, ((g + 1) // 2) % 2
    dz = 4 + (1 - 2 * (t % 2)) * ((t + 1) // 2)
    xh, z, c = me // 16, (me // 2) % 8, me % 2
    return ((xh + dx) % 2) * 16 + ((z + dz) % 8) * 2 + (c + dc) % 2


def greet(me_s, me_d):
    barrier = pltpu.get_barrier_semaphore()

    def over_seq(k, carry):
        pl.semaphore_signal(barrier, inc=1, device_id={"seq": seq_peer(k, me_s)}, device_id_type=MESH)
        return carry

    def over_dp(k, carry):
        pl.semaphore_signal(barrier, inc=1, device_id={"dp": lax.rem(me_d + k, ND)}, device_id_type=MESH)
        return carry

    lax.fori_loop(0, NS - 1, over_seq, 0)
    lax.fori_loop(1, ND, over_dp, 0)
    pl.semaphore_wait(barrier, NS - 1 + ND - 1)


def a2a_start(sbuf, rbuf, ssem, rsem, me):
    def send(k, carry):
        peer = seq_peer(k, me)
        remote(sbuf.at[peer], rbuf.at[me], ssem, rsem, {"seq": peer}).start()
        return carry

    lax.fori_loop(0, NS - 1, send, 0)
    rbuf[me] = sbuf[me]


def a2a_recv(sbuf, rbuf, ssem, rsem, me):
    part = pl.ds(0, NS - 1)
    remote(sbuf.at[part], rbuf.at[part], ssem, rsem, {"seq": me}).wait_recv()


def a2a_sent(sbuf, rbuf, ssem, rsem, me):
    part = pl.ds(0, NS - 1)
    remote(sbuf.at[part], rbuf.at[part], ssem, rsem, {"seq": me}).wait_send()


def tiles(rows, tile, body):
    def step(t, carry):
        body(pl.ds(pl.multiple_of(t * tile, tile), tile), t)
        return carry

    lax.fori_loop(0, rows // tile, step, 0)


def blk(n, width=DB):
    return slice(n * width, (n + 1) * width)


def unpack_lanes(packed, store):
    count = packed.shape[0]
    for t in range(3):
        v = packed[:, :, 128 * t : 128 * t + 128].astype(F32).reshape(count, 2, 8, 128)
        store(256 * t, v[:, 0].reshape(count * 8, 128))
        store(256 * t + 128, v[:, 1].reshape(count * 8, 128))


def pack_pair(low, high):
    count = low.shape[0] // 8
    both = jnp.concatenate([low.reshape(count, 8, -1), high.reshape(count, 8, -1)], axis=1)
    return both.astype(BF16)


def factor_of(rows):
    return lax.rsqrt(jnp.mean(rows * rows, axis=-1, keepdims=True) + EPS)


def fold_rows(product, acc):
    for r in range(product.shape[0] // 8):
        acc = acc + product[8 * r : 8 * r + 8]
    return acc


def gelu_pair(h):
    size = jnp.abs(h)
    den = 1.0 + (0.3275911 / math.sqrt(2.0)) * size
    t = pl.reciprocal(den, approx=True)
    t = t * (2.0 - den * t)
    e = jnp.exp(-0.5 * (h * h))
    poly = 0.5 * 1.061405429
    for a in (-1.453152027, 1.421413741, -0.284496736, 0.254829592):
        poly = poly * t + 0.5 * a
    q = poly * t * e
    cdf = jnp.where(h >= 0.0, 1.0 - q, q)
    return h * cdf, cdf + h * (e * (1.0 / math.sqrt(2.0 * math.pi)))


def main_kernel(
    x_ref, cot_ref, g1_ref, g2_ref, vw_ref, gw_ref, ow_ref, up_ref, dn_ref, fb_ref, sb_ref,
    pm_ref, ex_ref, p3_ref, p12_ref,
    out_ref, gin_ref, gfirst_ref, gsecond_ref, early_ref, late_ref,
    n1, val, gate, mixed, y, mid, n2, dmid, dgate, df, dval, act, dpre, dact, mm, dmu, t768, hbuf,
    s1, r1, s2, r2, s3, r3, s4, r4, ars, arr, ag, gsec, gain2, tmp,
    ssem, rsem,
):
    me_s, me_d = lax.axis_index("seq"), lax.axis_index("dp")
    greet(me_s, me_d)
    g1, g2 = g1_ref[...], g2_ref[...]

    def norm_first(rows, t):
        v = x_ref[rows, :].astype(F32)
        n1[rows, :] = (v * factor_of(v) * g1).astype(BF16)

    tiles(ROWS, 32, norm_first)
    for n in range(NB):
        val[:, blk(n)] = dot(n1[:, blk(n)], vw_ref[:, blk(n)]).astype(BF16)
    for ct in range(3):
        lanes = slice(256 * ct, 256 * ct + 256)
        pair = [dot(fb_ref[ii], val[ii * HALF : (ii + 1) * HALF, lanes]) for ii in range(2)]
        s1[:, :, lanes] = pack_pair(*pair)
    a2a_start(s1, r1, ssem.at[0], rsem.at[0], me_s)

    for n in range(NB):
        gate[:, blk(n)] = dot(n1[:, blk(n)], gw_ref[:, blk(n)]).astype(BF16)
    spread = dot(pm_ref[...], sb_ref[...]).astype(BF16)
    for ii in range(2):
        wide = dot(spread[ii * HALF : (ii + 1) * HALF], ex_ref[...])
        same = (lax.broadcasted_iota(jnp.int32, wide.shape, 0) & 7) == (
            lax.broadcasted_iota(jnp.int32, wide.shape, 1) & 7
        )
        mm[ii] = jnp.where(same, wide, 0.0).astype(BF16)
    for n in range(NB):
        for ii in range(2):
            dact[ii, n] = dot(cot_ref[ii * HALF : (ii + 1) * HALF, blk(n)], dn_ref[:, blk(n)], 1, 1)

    a2a_recv(s1, r1, ssem.at[0], rsem.at[0], me_s)
    for ii in range(2):
        for ct in range(3):
            lanes = slice(256 * ct, 256 * ct + 256)
            o = dot(mm[ii], r1[:, :, lanes].reshape(NS * 16, 256))
            s2[ii, :, :, 128 * ct : 128 * ct + 128] = pack_pair(o[:, :128], o[:, 128:])
        a2a_start(s2.at[ii], r2.at[ii], ssem.at[1 + ii], rsem.at[1 + ii], me_s)

    gain2[...] = jnp.zeros_like(gain2)

    def token_half(ii, carry):
        base = ii * HALF
        half = pl.ds(pl.multiple_of(base, HALF), HALF)

        def rows_of(rows):
            return pl.ds(pl.multiple_of(base + rows.start, rows.size), rows.size)

        a2a_recv(s2.at[ii], r2.at[ii], ssem.at[1 + ii], rsem.at[1 + ii], me_s)

        def gated(rows, t):
            part = r2[ii, pl.ds(pl.multiple_of(t * 4, 4), 4)]

            def store(lane, v):
                at = (rows_of(rows), slice(lane, lane + 128))
                mixed[at] = v.astype(BF16)
                y[at] = (v * gate[at].astype(F32)).astype(BF16)

            unpack_lanes(part, store)

        tiles(HALF, 32, gated)
        for n in range(NB):
            t768[:, blk(n)] = dot(y[half, blk(n)], ow_ref[:, blk(n)])

        def norm_second(rows, t):
            m = (x_ref[rows_of(rows), :].astype(F32) + t768[rows, :]).astype(BF16)
            mid[rows_of(rows), :] = m
            mf = m.astype(F32)
            n2[rows_of(rows), :] = (mf * factor_of(mf) * g2).astype(BF16)

        tiles(HALF, 32, norm_second)
        for n in range(NB):
            hbuf[...] = dot(n2[half, blk(n)], up_ref[:, blk(n, HB)])

            def gelu(rows, t):
                for lt in range(3):
                    lanes = slice(256 * lt, 256 * lt + 256)
                    wide = slice(n * HB + 256 * lt, n * HB + 256 * lt + 256)
                    value, slope = gelu_pair(hbuf[rows, lanes])
                    act[rows_of(rows), wide] = value.astype(BF16)
                    dpre[rows_of(rows), wide] = (slope * dact[ii, n, rows, lanes]).astype(BF16)

            tiles(HALF, 32, gelu)
            t768[:, blk(n)] = dot(dpre[half, blk(n, HB)], up_ref[:, blk(n, HB)], 1, 1)

        def norm_back_second(rows, t):
            mf = mid[rows_of(rows), :].astype(F32)
            f2 = factor_of(mf)
            u2 = mf * f2
            h2 = t768[rows, :]
            gain2[...] = fold_rows(h2 * u2, gain2[...])
            s = h2 * g2
            d = cot_ref[rows_of(rows), :].astype(F32) + f2 * (s - u2 * jnp.mean(s * u2, axis=-1, keepdims=True))
            dmid[rows_of(rows), :] = d.astype(BF16)

        tiles(HALF, 32, norm_back_second)
        for n in range(NB):
            t768[:, blk(n)] = dot(dmid[half, blk(n)], ow_ref[:, blk(n)], 1, 1)

        def gates_back(rows, t):
            dy = t768[rows, :]
            at = rows_of(rows)
            dgate[at, :] = (dy * mixed[at, :].astype(F32)).astype(BF16)
            dm = dy * gate[at, :].astype(F32)
            for ct in range(3):
                low, high = dm[:, 256 * ct : 256 * ct + 128], dm[:, 256 * ct + 128 : 256 * ct + 256]
                s3[ii, pl.ds(pl.multiple_of(t * 4, 4), 4), :, 128 * ct : 128 * ct + 128] = pack_pair(low, high)

        tiles(HALF, 32, gates_back)
        a2a_start(s3.at[ii], r3.at[ii], ssem.at[3 + ii], rsem.at[3 + ii], me_s)
        return carry

    lax.fori_loop(0, 2, token_half, 0)

    for n in range(NB):
        t = dot(act[:, blk(n, HB)], dn_ref[:, blk(n)])
        out_ref[:, blk(n)] = (mid[:, blk(n)].astype(F32) + t).astype(BF16)
    gain2_t = gain2[...].T
    for n in range(NB):
        tmp[:, 0:D] = dot(cot_ref[:, blk(n)], act[:, blk(n, HB)], 0, 0).astype(BF16)
        tmp[:, D : D + DB] = dot(dgate[:, blk(n)], n1[:, blk(n)], 0, 0).astype(BF16)
        tmp[:, D + DB : GL] = dot(dmid[:, blk(n)], y[:, blk(n)], 0, 0).astype(BF16)
        tmp[:, GL:UL] = jnp.concatenate([gain2_t[blk(n)], jnp.zeros((DB, 120), F32)], axis=1).astype(BF16)
        moved = dot(p3_ref[...], tmp[...]).astype(BF16)
        early_ref[0, n, :, 0:UL] = moved[:96]
        early_ref[1, n, :, 0:UL] = moved[96:]
        grad_up = dot(dpre[:, blk(n, HB)], n2[:, blk(n)], 0, 0).astype(BF16)
        for q in range(4):
            moved = dot(p12_ref[...], grad_up[blk(q)]).astype(BF16)
            early_ref[0, n, :, UL + DB * q : UL + DB * q + DB] = moved[:96]
            early_ref[1, n, :, UL + DB * q : UL + DB * q + DB] = moved[96:]

    for ii in range(2):
        a2a_recv(s3.at[ii], r3.at[ii], ssem.at[3 + ii], rsem.at[3 + ii], me_s)

        def unpack(rows, t):
            def store(lane, v):
                dmu[pl.ds(pl.multiple_of(ii * HALF + t * 32, 32), 32), lane : lane + 128] = v.astype(BF16)

            unpack_lanes(r3[ii, pl.ds(pl.multiple_of(t * 4, 4), 4)], store)

        tiles(HALF, 32, unpack)
    for ct in range(3):
        lanes = slice(256 * ct, 256 * ct + 256)
        o = dot(mm[...].reshape(ROWS, ROWS), dmu[:, lanes], 0, 0)
        s4[:, :, lanes] = o.astype(BF16).reshape(NS, 16, 256)
    a2a_start(s4, r4, ssem.at[5], rsem.at[5], me_s)
    for ii in range(2):
        g = dot(dmu[ii * HALF : (ii + 1) * HALF, :], r1[...].reshape(ROWS, D), 1, 1) * MIX_SCALE
        same = (lax.broadcasted_iota(jnp.int32, g.shape, 0) & 7) == (
            lax.broadcasted_iota(jnp.int32, g.shape, 1) & 7
        )
        g = dot(jnp.where(same, g, 0.0).astype(BF16), ex_ref[...], 1, 1)
        gsec[:, 64 * ii : 64 * ii + 64] = g.astype(BF16)

    a2a_recv(s4, r4, ssem.at[5], rsem.at[5], me_s)
    for ct in range(3):
        lanes = slice(256 * ct, 256 * ct + 256)
        v = r4[:, :, lanes].astype(F32).reshape(NS, 2, 8, 256)
        for ii in range(2):
            df[ii * HALF : (ii + 1) * HALF, lanes] = v[:, ii].reshape(HALF, 256).astype(BF16)
    for ii in range(2):
        half = slice(ii * HALF, (ii + 1) * HALF)
        g = (dot(df[half, :], val[half, :], 1, 1) * MIX_SCALE).astype(BF16)
        for part in range(4):
            ars[4 * ii + part, 0:64, :] = g[64 * part : 64 * part + 64]
    for part in range(ND):
        ars[part, 64:80, 0:128] = gsec[32 * part : 32 * part + 16, :]
        ars[part, 64:80, 128:256] = gsec[32 * part + 16 : 32 * part + 32, :]

    def reduce_send(k, carry):
        peer = lax.rem(me_d + k, ND)
        remote(ars.at[peer], arr.at[me_d], ssem.at[6], rsem.at[6], {"dp": peer}).start()
        return carry

    lax.fori_loop(1, ND, reduce_send, 0)
    arr[me_d] = ars[me_d]

    for ii in range(2):
        half = slice(ii * HALF, (ii + 1) * HALF)
        dval[half, :] = dot(fb_ref[ii], df[half, :], 0, 0).astype(BF16)

    others = pl.ds(0, ND - 1)
    remote(ars.at[others], arr.at[others], ssem.at[6], rsem.at[6], {"dp": me_d}).wait_recv()
    total = arr[0].astype(F32)
    for k in range(1, ND):
        total = total + arr[k].astype(F32)
    ag[me_d] = total.astype(BF16)

    def gather_send(k, carry):
        peer = lax.rem(me_d + k, ND)
        remote(ag.at[me_d], ag.at[me_d], ssem.at[7], rsem.at[7], {"dp": peer}).start()
        return carry

    lax.fori_loop(1, ND, gather_send, 0)

    for n in range(NB):
        for ii in range(2):
            half = slice(ii * HALF, (ii + 1) * HALF)
            dact[ii, 0, :, blk(n)] = dot(dval[half, blk(n)], vw_ref[:, blk(n)], 1, 1) + dot(
                dgate[half, blk(n)], gw_ref[:, blk(n)], 1, 1
            )
    gain2[...] = jnp.zeros_like(gain2)
    for ii in range(2):

        def norm_back_first(rows, t):
            at = pl.ds(pl.multiple_of(ii * HALF + t * 32, 32), 32)
            v = x_ref[at, :].astype(F32)
            f1 = factor_of(v)
            u1 = v * f1
            h1 = dact[ii, 0, rows, :]
            gain2[...] = fold_rows(h1 * u1, gain2[...])
            s = h1 * g1
            d = dmid[at, :].astype(F32) + f1 * (s - u1 * jnp.mean(s * u1, axis=-1, keepdims=True))
            gin_ref[at, :] = d.astype(BF16)

        tiles(HALF, 32, norm_back_first)
    gain1_t = gain2[...].T
    for n in range(NB):
        grad_v = dot(dval[:, blk(n)], n1[:, blk(n)], 0, 0)
        piece = jnp.concatenate([grad_v, gain1_t[blk(n)], jnp.zeros((DB, 56), F32)], axis=1).astype(BF16)
        moved = dot(p3_ref[...], piece).astype(BF16)
        late_ref[0, n] = moved[:96]
        late_ref[1, n] = moved[96:]

    remote(ag.at[others], ag.at[others], ssem.at[7], rsem.at[7], {"dp": me_d}).wait_recv()
    for part in range(ND):
        ii, at = part // 4, 64 * (part % 4)
        gfirst_ref[ii, at : at + 64, :] = ag[part, 0:64, :].astype(F32)
        dmu[32 * part : 32 * part + 16, 0:128] = ag[part, 64:80, 0:128]
        dmu[32 * part + 16 : 32 * part + 32, 0:128] = ag[part, 64:80, 128:256]
    gsecond_ref[...] = dot(pm_ref[0:HALF, :], dmu[0:HALF, 0:64], 0, 0) + dot(
        pm_ref[HALF:ROWS, :], dmu[0:HALF, 64:128], 0, 0
    )

    a2a_sent(s1, r1, ssem.at[0], rsem.at[0], me_s)
    for ii in range(2):
        a2a_sent(s2.at[ii], r2.at[ii], ssem.at[1 + ii], rsem.at[1 + ii], me_s)
        a2a_sent(s3.at[ii], r3.at[ii], ssem.at[3 + ii], rsem.at[3 + ii], me_s)
    a2a_sent(s4, r4, ssem.at[5], rsem.at[5], me_s)
    remote(ars.at[others], arr.at[others], ssem.at[6], rsem.at[6], {"dp": me_d}).wait_send()
    remote(ag.at[others], ag.at[others], ssem.at[7], rsem.at[7], {"dp": me_d}).wait_send()


def reduce_kernel(
    early_ref, late_ref, fold_ref, ufold_ref,
    gv_ref, gg_ref, go_ref, gu_ref, gd_ref, g1_ref, g2_ref,
    core_e, core_l, ys_e, ys_l, yr_e, yr_l, xs_d, xs_u, xs_l, xr_d, xr_u, xr_l, fs, fr, fsl, frl, full, full_l,
    ssem, rsem,
):
    me_s, me_d = lax.axis_index("seq"), lax.axis_index("dp")
    greet(me_s, me_d)
    yy, xl = me_d // NXL, lax.rem(me_d, NXL)
    hz, core = me_s // NC, lax.rem(me_s, NC)
    mate = {"seq": hz * NC + 1 - core}

    first = [
        remote(early_ref.at[1 - core], core_e, ssem.at[0], rsem.at[0], mate),
        remote(late_ref.at[1 - core], core_l, ssem.at[1], rsem.at[1], mate),
    ]
    for copy in first:
        copy.start()
    for copy in first:
        copy.wait_recv()
    for n in range(NY):
        ys_e[n] = (early_ref[core, n].astype(F32) + core_e[n].astype(F32)).astype(BF16)
        ys_l[n] = (late_ref[core, n].astype(F32) + core_l[n].astype(F32)).astype(BF16)

    def y_send(k, carry):
        to = lax.rem(yy + k, NY)
        peer = {"dp": to * NXL + xl}
        remote(ys_e.at[to], yr_e.at[yy], ssem.at[2], rsem.at[2], peer).start()
        remote(ys_l.at[to], yr_l.at[yy], ssem.at[3], rsem.at[3], peer).start()
        return carry

    lax.fori_loop(1, NY, y_send, 0)
    yr_e[yy] = ys_e[yy]
    yr_l[yy] = ys_l[yy]
    part = pl.ds(0, NY - 1)
    y_all = [
        remote(ys_e.at[part], yr_e.at[part], ssem.at[2], rsem.at[2], mate),
        remote(ys_l.at[part], yr_l.at[part], ssem.at[3], rsem.at[3], mate),
    ]
    for copy in y_all:
        copy.wait_recv()
    total = yr_e[0].astype(F32)
    total_l = yr_l[0].astype(F32)
    for k in range(1, NY):
        total = total + yr_e[k].astype(F32)
        total_l = total_l + yr_l[k].astype(F32)
    full[...] = total
    full_l[...] = total_l

    for h in range(NXL):
        xs_d[h] = full[48 * h : 48 * h + 48, 0:UL].astype(BF16)
        xs_u[h] = full[:, UL + 384 * h : UL + 384 * h + 384].astype(BF16)
        xs_l[h] = full_l[48 * h : 48 * h + 48, :].astype(BF16)
    beside = {"dp": yy * NXL + 1 - xl}
    second = [
        remote(xs_d.at[1 - xl], xr_d, ssem.at[4], rsem.at[4], beside),
        remote(xs_u.at[1 - xl], xr_u, ssem.at[5], rsem.at[5], beside),
        remote(xs_l.at[1 - xl], xr_l, ssem.at[6], rsem.at[6], beside),
    ]
    for copy in second:
        copy.start()
    for copy in second:
        copy.wait_recv()
    dd = (xs_d[xl].astype(F32) + xr_d[...].astype(F32)).astype(BF16)
    uu = (xs_u[xl].astype(F32) + xr_u[...].astype(F32)).astype(BF16)
    ll = (xs_l[xl].astype(F32) + xr_l[...].astype(F32)).astype(BF16)

    folded = dot(fold_ref[:, 0:48], dd[:, 0:512]) + dot(fold_ref[:, 48:96], dd[:, 512:1024])
    fs[:, :, :] = folded.astype(BF16).reshape(16, 16, 512)
    tail = dot(fold_ref[:, 96:144], dd[:, 1024:1280]).astype(BF16).reshape(16, 16, 256)
    fs[:, :, 0:256] = fs[:, :, 0:256] + tail
    for h in range(NXH):
        u = uu[:, DB * h : DB * h + DB]
        low = dot(ufold_ref[:, 0:96], u).astype(BF16).reshape(8, 16, DB)
        high = dot(ufold_ref[:, 96:192], u).astype(BF16).reshape(8, 16, DB)
        at = slice(8 * h, 8 * h + 8)
        fs[at, :, 0:DB] = fs[at, :, 0:DB] + low
        fs[at, :, 256 : 256 + DB] = fs[at, :, 256 : 256 + DB] + high
    fsl[...] = dot(fold_ref[:, 0:48], ll).astype(BF16).reshape(16, 16, LW)

    def last_send(k, carry):
        to = lax.rem(hz + k, NXH * NZ)
        peer = {"seq": to * NC + core}
        remote(fs.at[to], fr.at[hz], ssem.at[7], rsem.at[7], peer).start()
        remote(fsl.at[to], frl.at[hz], ssem.at[8], rsem.at[8], peer).start()
        return carry

    lax.fori_loop(1, NXH * NZ, last_send, 0)
    fr[hz] = fs[hz]
    frl[hz] = fsl[hz]
    part = pl.ds(0, NXH * NZ - 1)
    last = [
        remote(fs.at[part], fr.at[part], ssem.at[7], rsem.at[7], mate),
        remote(fsl.at[part], frl.at[part], ssem.at[8], rsem.at[8], mate),
    ]
    for copy in last:
        copy.wait_recv()
    total = fr[0].astype(F32)
    total_l = frl[0].astype(F32)
    for k in range(1, NXH * NZ):
        total = total + fr[k].astype(F32)
        total_l = total_l + frl[k].astype(F32)
    across = (total * ROW_SCALE).T
    across_l = (total_l * ROW_SCALE).T
    gd_ref[0:512, :] = across[0:512, 0:3]
    gd_ref[512:768, :] = across[0:256, 3:6]
    gg_ref[...] = across[256:448, 3:6]
    go_ref[0:64, :] = across[448:512, 3:6]
    go_ref[64:192, :] = across[0:128, 6:9]
    gu_ref[:, 0:6] = across[0:192, 9:15]
    gu_ref[:, 6:12] = across[256:448, 9:15]
    g2_ref[...] = jnp.sum(across[128:136, 6:9], axis=0, keepdims=True)
    gv_ref[...] = across_l[0:192, 0:3]
    g1_ref[...] = jnp.sum(across_l[192:200, 0:3], axis=0, keepdims=True)

    for copy in first + y_all + second + last:
        copy.wait_send()


def vmem_specs(count):
    return [pl.BlockSpec(memory_space=pltpu.VMEM)] * count


def body(inputs, cotangent, gain_first, gain_second, value_w, gate_w, out_w, up_w, down_w, first_blocks, second_blocks):
    perm_m, expand, perm3, perm12, fold, ufold = [jnp.asarray(a, BF16) for a in constants()]
    shape = jax.ShapeDtypeStruct
    vm = lambda *s: pltpu.VMEM(s, BF16)
    vf = lambda *s: pltpu.VMEM(s, F32)
    big = lambda: vm(ROWS, D)
    out, gin, gfirst, gsecond, early, late = pl.pallas_call(
        main_kernel,
        out_shape=[
            shape((ROWS, D), BF16), shape((ROWS, D), BF16), shape((2, 256, 256), F32), shape((512, 64), F32),
            shape((2, NB, 96, EW), BF16), shape((2, NB, 96, LW), BF16),
        ],
        in_specs=vmem_specs(15),
        out_specs=vmem_specs(6),
        scratch_shapes=[
            big(), big(), big(), big(), big(), big(), big(), big(), big(), big(), big(),
            vm(ROWS, NB * HB), vm(ROWS, NB * HB), vf(2, NB, HALF, HB),
            vm(2, HALF, ROWS), big(), vf(HALF, D), vf(HALF, HB),
            vm(NS, 16, D), vm(NS, 16, D), vm(2, NS, 16, 384), vm(2, NS, 16, 384),
            vm(2, NS, 16, 384), vm(2, NS, 16, 384), vm(NS, 16, D), vm(NS, 16, D),
            vm(ND, 80, 256), vm(ND, 80, 256), vm(ND, 80, 256), vm(HALF, 128),
            vf(8, D), vm(DB, UL),
            pltpu.SemaphoreType.DMA((8,)), pltpu.SemaphoreType.DMA((8,)),
        ],
        compiler_params=pltpu.CompilerParams(
            collective_id=0, has_side_effects=True, vmem_limit_bytes=VMEM_LIMIT
        ),
    )(
        inputs.reshape(ROWS, D), cotangent.reshape(ROWS, D), gain_first.reshape(1, D), gain_second.reshape(1, D),
        value_w, gate_w, out_w, up_w, down_w, first_blocks, second_blocks.reshape(512, 64),
        perm_m, expand, perm3, perm12,
    )
    gv, gg, go, gu, gd, g1, g2 = pl.pallas_call(
        reduce_kernel,
        out_shape=[
            shape((DB, 3), F32), shape((DB, 3), F32), shape((DB, 3), F32), shape((DB, 12), F32), shape((HB, 3), F32),
            shape((1, 3), F32), shape((1, 3), F32),
        ],
        in_specs=vmem_specs(4),
        out_specs=vmem_specs(7),
        scratch_shapes=[
            vm(NY, 96, EW), vm(NY, 96, LW), vm(NY, 96, EW), vm(NY, 96, LW), vm(NY, 96, EW), vm(NY, 96, LW),
            vm(2, 48, UL), vm(2, 96, 384), vm(2, 48, LW), vm(48, UL), vm(96, 384), vm(48, LW),
            vm(16, 16, 512), vm(16, 16, 512), vm(16, 16, LW), vm(16, 16, LW), vf(96, EW), vf(96, LW),
            pltpu.SemaphoreType.DMA((9,)), pltpu.SemaphoreType.DMA((9,)),
        ],
        compiler_params=pltpu.CompilerParams(
            collective_id=1, has_side_effects=True, vmem_limit_bytes=VMEM_LIMIT
        ),
    )(early, late, fold, ufold)
    return (
        out.reshape(1, ROWS, D), gin.reshape(1, ROWS, D), gv, gg, go, gu, gd, g1.reshape(3), g2.reshape(3),
        gfirst, gsecond.reshape(8, 64, 64),
    )


def solution(mesh):
    tokens, whole = P("dp", "seq", None), P("seq", None, None)
    columns = P(None, ("dp", "seq"))
    gains = P(("dp", "seq"))
    return jax.shard_map(
        body,
        mesh=mesh,
        in_specs=(tokens, tokens, P(), P(), P(), P(), P(), P(), P(), whole, whole),
        out_specs=(tokens, tokens, columns, columns, columns, columns, columns, gains, gains, whole, whole),
        check_vma=False,
    )
```

time: 574 us -> 178 us (0.31)
  waiting for transfers between devices: 272 us -> 0 us
  Pallas kernels: 0 us -> 162 us
  blocking collectives: 141 us -> 0 us
  local copies, waits for them, and re-layouts: 69 us -> 15 us
  matrix products: 52.8 us -> 0 us
  between operations: 14.5 us -> 0.7 us
  starting transfers between devices: 13.1 us -> 0 us
  other arithmetic: 10.2 us -> 0 us
    unnamed x3 -> x0, waiting for transfers between devices: 247 us -> none
    pallas_call x0 -> x2, Pallas kernels: none -> 162 us  [the longest x1 109 us: body(): pl.pallas_call(main_kernel, out_shape=[shape((ROWS, D), BF16), shape((ROW...]
    unnamed x1 -> x0, blocking collectives: 76.6 us -> none
    all_to_all x2 -> x0, blocking collectives: 64 us -> none  [to_columns(): lax.all_to_all(grid_rows, 'seq', split_axis=2, concat_axis=1, tiled=True)]
    dot_general x21 -> x0, matrix products: 52.8 us -> none  [the longest x5 25.8 us: blocked(): jnp.einsum('rnd,dne->rne', split, wide_w, preferred_element_type=jnp.floa...]
    convert_element_type x11 -> x0, local copies, waits for them, and re-layouts: 25.1 us -> none  [the longest x2 6.82 us: body(): d_mixed = (d_y * gate_rows.astype(jnp.float32)).astype(jnp.bfloat16)]
    all_to_all x2 -> x0, waiting for transfers between devices: 24.4 us -> none  [to_rows(): lax.all_to_all(grid_cols, 'seq', split_axis=1, concat_axis=2, tiled=True)]
    all_to_all x2 -> x0, starting transfers between devices: 13 us -> none  [to_rows(): lax.all_to_all(grid_cols, 'seq', split_axis=1, concat_axis=2, tiled=True)]
  transfers between devices with their start and end apart: 4 -> 0, of which waited for: 3 -> 0; matrix products, arithmetic and copies ran while one was open for 10% -> 0% of each run, Pallas kernels for 0% -> 0%
where the time goes in v1:
time: 178 us
  Pallas kernels  162 us (91%)
  local copies, waits for them, and re-layouts  15 us (8%)
    pallas_call x1, Pallas kernels, body(): pl.pallas_call(main_kernel, out_shape=[shape((ROWS, D), BF16), shape((ROW...  109 us
    pallas_call x1, Pallas kernels, body(): pl.pallas_call(reduce_kernel, out_shape=[shape((DB, 3), F32), shape((DB,...  53.1 us
    unnamed x23, local copies, waits for them, and re-layouts  12.4 us

profile of v1, /device:TPU:1, one launch (start us, length us, event | category | flops | bytes accessed | tf_op | source)
XLA Modules:
  0.0 177.8 jit_solution(13446991338592876412)
XLA Ops:
  0.6 1.3 reshape.54.g1_ref
  1.9 1.3 reshape.55.g2_ref
  3.2 109.0 %shard_map.248 = (bf16[512,768]{1,0:T(8,128)(2,1)}, bf16[512,768]{1,0:T(8,128)(2,1)}, f32[2,256,256]{2,1,0:T(8,128)}, f32[512,64]{1,0:T(8,128)}, bf16[2,4,96,204...) custom-call(bf16[512,768]{1,0:T(8,128)(2,1)} %bitcast.8, bf16[512,768]{1,0:T(8,128)(2,1)} %bitcast.9, ...), custom_call_target="tpu_custom_call" | custom-call | tf_op jit(solution)/shard_map/pallas_call | solution.py:544
  112.2 53.1 %shard_map.249 = (f32[192,3]{1,0:T(8,128)}, f32[192,3]{1,0:T(8,128)}, f32[192,3]{1,0:T(8,128)}, f32[192,12]{1,0:T(8,128)}, f32[768,3]{1,0:T(8,128)}, /*index=5*/f32[1,3]{1,0:T(1,128)}, f32[1,3]{1,0:T(1,128)}) custom-call(bf16[2,4,96,2048]{3,2,1,0:T(8,128)(2,1)} %get-tuple-element.26.early_ref, bf16[2,4,96,256]{3,2,1,0:T(8,128)(2,1)} %get-tuple-element.27.late_ref, ...), custom_call_target="tpu_custom_call" | custom-call | tf_op jit(solution)/shard_map/pallas_call | solution.py:570
  165.3 0.0 copy-start.1
  165.3 0.0 copy-start
  165.3 1.7 copy.28
  167.0 1.6 copy.29
  168.6 1.6 copy.30
  170.1 1.7 copy.32
  171.9 1.6 copy.31
  173.5 0.0 copy-done.1
  173.5 0.9 copy.39
  174.3 0.0 copy-done
  174.3 0.0 copy-start.5
  174.4 0.0 copy-start.4
  174.4 0.0 copy-start.2
  174.4 0.0 copy-start.3
  174.4 0.9 copy.40
  175.2 0.0 copy-done.5
  175.3 0.5 copy.41
  175.8 0.0 copy-done.4
  175.8 0.5 copy.42
  176.3 0.0 copy-done.2
  176.3 0.8 copy.43
  177.1 0.0 copy-done.3
  177.1 0.7 copy.44
Async XLA Ops:
  165.3 8.2 %copy-start.1 = (bf16[512,768]{1,0:T(8,128)(2,1)S(1)}, bf16[512,768]{1,0:T(8,128)(2,1)}, u32[]{:S(2)}) copy-start(bf16[512,768]{1,0:T(8,128)(2,1)} %get-tuple-element.24) | copy-start | bytes 2359300
  165.3 9.0 %copy-start = (bf16[512,768]{1,0:T(8,128)(2,1)S(1)}, bf16[512,768]{1,0:T(8,128)(2,1)}, u32[]{:S(2)}) copy-start(bf16[512,768]{1,0:T(8,128)(2,1)} %get-tuple-element.25) | copy-start | bytes 2359300
  174.3 0.9 copy-start.5
  174.4 1.4 copy-start.4
  174.4 1.9 %copy-start.2 = (f32[2,256,256]{2,1,0:T(8,128)S(1)}, f32[2,256,256]{2,1,0:T(8,128)}, u32[]{:S(2)}) copy-start(f32[2,256,256]{2,1,0:T(8,128)} %get-tuple-element.68) | copy-start | bytes 1572868
  174.4 2.7 %copy-start.3 = (f32[512,64]{1,0:T(8,128)S(1)}, f32[512,64]{1,0:T(8,128)}, u32[]{:S(2)}) copy-start(f32[512,64]{1,0:T(8,128)} %get-tuple-element.36) | copy-start | bytes 393220

commit v2 on v1

v2 whole, which is shorter than its diff:
```python
import functools
import math

import jax
import jax.numpy as jnp
import numpy as np
from jax import lax
from jax.experimental import pallas as pl
from jax.experimental.pallas import tpu as pltpu
from jax.sharding import PartitionSpec as P

MESH = pl.DeviceIdType.MESH
F32 = jnp.float32
BF16 = jnp.bfloat16
EPS = 1e-6
NY, NXL, NXH, NZ, NC = 4, 2, 2, 8, 2
NS, ND = NXH * NZ * NC, NY * NXL
D, NB, DB, HB, ROWS, HALF = 768, 4, 192, 768, 512, 256
ROW_SCALE = 1.0 / math.sqrt(131072.0)
MIX_SCALE = 1.0 / math.sqrt(6144.0)
DL, UL, LW = 1280, 768, 256
GL = 1152
A1, A2, A2B, A3, A3B, A4, GS, GF, CORE, YY, XX, LAST = 0, 3, 6, 7, 8, 11, 14, 16, 18, 21, 24, 27
SEMS = 29
VMEM_LIMIT = 60 * 2**20


def dot(a, b, ca=1, cb=0):
    return lax.dot_general(a, b, (((ca,), (cb,)), ((), ())), preferred_element_type=F32)


def constants():
    one = lambda shape, pairs: _onehot(shape, pairs)
    row, col = [], []
    for ii in range(2):
        for d in range(NS):
            for bl in range(8):
                row.append(ii * 256 + d * 8 + bl)
                col.append(bl * 64 + 2 * d + ii)
    perm_m = one((512, 512), (row, col))
    expand = one((64, 512), (np.arange(512) // 8, np.arange(512)))
    out = np.arange(192)
    c, rem = out // 96, out % 96
    perm3 = one((192, 192), (out, rem // 3 * 6 + c * 3 + rem % 3))
    perm12 = one((192, 192), (out, rem // 12 * 24 + c * 12 + rem % 12))
    dest, t = np.arange(48) // 3, np.arange(48) % 3
    fold = np.concatenate([one((256, 48), (dest * 16 + 3 * f + t, np.arange(48))) for f in range(3)], axis=1)
    z, t = np.arange(96) // 12, np.arange(96) % 12
    low, high = t < 6, t >= 6
    ufold = np.concatenate(
        [
            one((128, 96), ((z * 16 + 9 + t)[low], np.arange(96)[low])),
            one((128, 96), ((z * 16 + 3 + t)[high], np.arange(96)[high])),
        ],
        axis=1,
    )
    return perm_m, expand, perm3, perm12, fold, ufold


def _onehot(shape, pairs):
    array = np.zeros(shape, np.float32)
    array[pairs[0], pairs[1]] = 1.0
    return array


def remote(src, dst, ssem, rsem, device):
    return pltpu.make_async_remote_copy(
        src_ref=src, dst_ref=dst, send_sem=ssem, recv_sem=rsem, device_id=device, device_id_type=MESH
    )


def seq_peer(k, me):
    g, t = k // 8, k % 8
    dx, dc = 1 - g // 2, ((g + 1) // 2) % 2
    dz = 4 + (1 - 2 * (t % 2)) * ((t + 1) // 2)
    xh, z, c = me // 16, (me // 2) % 8, me % 2
    return ((xh + dx) % 2) * 16 + ((z + dz) % 8) * 2 + (c + dc) % 2


def greet(me_s, me_d):
    barrier = pltpu.get_barrier_semaphore()

    def over_seq(k, carry):
        pl.semaphore_signal(barrier, inc=1, device_id={"seq": seq_peer(k, me_s)}, device_id_type=MESH)
        return carry

    def over_dp(k, carry):
        pl.semaphore_signal(barrier, inc=1, device_id={"dp": lax.rem(me_d + k, ND)}, device_id_type=MESH)
        return carry

    lax.fori_loop(0, NS - 1, over_seq, 0)
    lax.fori_loop(1, ND, over_dp, 0)
    return lambda: pl.semaphore_wait(barrier, NS - 1 + ND - 1)


class Exchange:
    def __init__(self, sbuf, rbuf, ssem, rsem, me, lanes=None):
        self.me, self.sems = me, (ssem, rsem)
        self.sbuf, self.rbuf, self.lanes = sbuf, rbuf, lanes

    def at(self, ref, index):
        return ref.at[index] if self.lanes is None else ref.at[index, :, self.lanes]

    def start(self):
        def send(k, carry):
            peer = seq_peer(k, self.me)
            remote(self.at(self.sbuf, peer), self.at(self.rbuf, self.me), *self.sems, {"seq": peer}).start()
            return carry

        lax.fori_loop(0, NS - 1, send, 0)
        if self.lanes is None:
            self.rbuf[self.me] = self.sbuf[self.me]
        else:
            self.rbuf[self.me, :, self.lanes] = self.sbuf[self.me, :, self.lanes]

    def whole(self):
        part = pl.ds(0, NS - 1)
        return remote(self.at(self.sbuf, part), self.at(self.rbuf, part), *self.sems, {"seq": self.me})

    def recv(self):
        self.whole().wait_recv()

    def sent(self):
        self.whole().wait_send()


class Ring:
    def __init__(self, sbuf, rbuf, ssem, rsem, me, count, device, same=False):
        self.sbuf, self.rbuf, self.sems = sbuf, rbuf, (ssem, rsem)
        self.me, self.count, self.device, self.same = me, count, device, same

    def start(self):
        def send(k, carry):
            to = lax.rem(self.me + k, self.count)
            source = self.sbuf.at[self.me if self.same else to]
            remote(source, self.rbuf.at[self.me], *self.sems, self.device(to)).start()
            return carry

        lax.fori_loop(1, self.count, send, 0)
        if not self.same:
            self.rbuf[self.me] = self.sbuf[self.me]

    def whole(self):
        part = pl.ds(0, self.count - 1)
        return remote(self.sbuf.at[part], self.rbuf.at[part], *self.sems, self.device(self.me))

    def recv(self):
        self.whole().wait_recv()

    def sent(self):
        self.whole().wait_send()

    def total(self):
        out = self.rbuf[0].astype(F32)
        for k in range(1, self.count):
            out = out + self.rbuf[k].astype(F32)
        return out


def tiles(rows, tile, body):
    def step(t, carry):
        body(pl.ds(pl.multiple_of(t * tile, tile), tile), t)
        return carry

    lax.fori_loop(0, rows // tile, step, 0)


def blk(n, width=DB):
    return slice(n * width, (n + 1) * width)


def unpack_lanes(packed, store):
    count = packed.shape[0]
    for t in range(3):
        v = packed[:, :, 128 * t : 128 * t + 128].astype(F32).reshape(count, 2, 8, 128)
        store(256 * t, v[:, 0].reshape(count * 8, 128))
        store(256 * t + 128, v[:, 1].reshape(count * 8, 128))


def pack_pair(low, high):
    count = low.shape[0] // 8
    both = jnp.concatenate([low.reshape(count, 8, -1), high.reshape(count, 8, -1)], axis=1)
    return both.astype(BF16)


def factor_of(rows):
    return lax.rsqrt(jnp.mean(rows * rows, axis=-1, keepdims=True) + EPS)


def fold_rows(product, acc):
    for r in range(product.shape[0] // 8):
        acc = acc + product[8 * r : 8 * r + 8]
    return acc


def gelu_pair(h):
    size = jnp.abs(h)
    den = 1.0 + (0.3275911 / math.sqrt(2.0)) * size
    t = pl.reciprocal(den, approx=True)
    t = t * (2.0 - den * t)
    e = jnp.exp(-0.5 * (h * h))
    poly = 0.5 * 1.061405429
    for a in (-1.453152027, 1.421413741, -0.284496736, 0.254829592):
        poly = poly * t + 0.5 * a
    q = poly * t * e
    cdf = jnp.where(h >= 0.0, 1.0 - q, q)
    return h * cdf, cdf + h * (e * (1.0 / math.sqrt(2.0 * math.pi)))


def same_block(shape):
    return (lax.broadcasted_iota(jnp.int32, shape, 0) & 7) == (lax.broadcasted_iota(jnp.int32, shape, 1) & 7)


def main_kernel(
    x_hbm, cot_hbm, g1_ref, g2_ref, vw_hbm, gw_hbm, ow_hbm, up_hbm, dn_hbm, fb_hbm, sb_hbm,
    pm_hbm, ex_hbm, p3_hbm, p12_hbm, fold_hbm, ufold_hbm,
    out_hbm, gin_hbm, mix_ref, early_ref, late_ref,
    x_ref, cot_ref, vw_ref, gw_ref, ow_ref, up_ref, dn_ref, fb_ref, sb_ref,
    pm_ref, ex_ref, p3_ref, p12_ref, fold_ref, ufold_ref, out_ref, gin_ref,
    n1, val, gate, mixed, y, mid, n2, dmid, dgate, df, dval, act, dpre, dact, mm, dmu, t768, hbuf, h1g, gfull,
    s1, r1, s2, r2, s3, r3, s4, r4, gss, gsr, gsa, gfs, gfr, gfa, gsec, gain2, gcol, tmp,
    cs_d, cs_u, cs_l, cr_d, cr_u, cr_l, ys_d, ys_u, ys_l, yr_d, yr_u, yr_l,
    xs_d, xs_u, xs_l, xr_d, xr_u, xr_l, fs, fr, fsl, frl,
    ssem, rsem, lsem,
):
    me_s, me_d = lax.axis_index("seq"), lax.axis_index("dp")
    yy, xl = me_d // NXL, lax.rem(me_d, NXL)
    hz, core = me_s // NC, lax.rem(me_s, NC)
    all_here = greet(me_s, me_d)

    def exchange(sbuf, rbuf, index, lanes=None):
        return Exchange(sbuf, rbuf, ssem.at[index], rsem.at[index], me_s, lanes)

    def lanes_of(ct, width=256):
        return slice(width * ct, width * ct + width)

    ex1 = [exchange(s1, r1, A1 + ct, lanes_of(ct)) for ct in range(3)]
    ex2 = [
        [exchange(s2.at[0], r2.at[0], A2 + ct, lanes_of(ct, 128)) for ct in range(3)],
        [exchange(s2.at[1], r2.at[1], A2B)],
    ]
    ex3 = [
        [exchange(s3.at[0], r3.at[0], A3)],
        [exchange(s3.at[1], r3.at[1], A3B + ct, lanes_of(ct, 128)) for ct in range(3)],
    ]
    ex4 = [exchange(s4, r4, A4 + ct, lanes_of(ct)) for ct in range(3)]

    def over_dp(sbuf, rbuf, index, same=False):
        return Ring(sbuf, rbuf, ssem.at[index], rsem.at[index], me_d, ND, lambda to: {"dp": to}, same)

    gs_sum, gs_all = over_dp(gss, gsr, GS), over_dp(gsa, gsa, GS + 1, True)
    gf_sum, gf_all = over_dp(gfs, gfr, GF), over_dp(gfa, gfa, GF + 1, True)
    pieces = ((cs_d, cr_d, ys_d, yr_d, xs_d, xr_d), (cs_u, cr_u, ys_u, yr_u, xs_u, xr_u), (cs_l, cr_l, ys_l, yr_l, xs_l, xr_l))
    mate, beside = {"seq": hz * NC + 1 - core}, {"dp": yy * NXL + 1 - xl}
    to_core = [remote(p[0].at[1 - core], p[1], ssem.at[CORE + i], rsem.at[CORE + i], mate) for i, p in enumerate(pieces)]
    to_y = [
        Ring(p[2], p[3], ssem.at[YY + i], rsem.at[YY + i], yy, NY, lambda to: {"dp": to * NXL + xl})
        for i, p in enumerate(pieces)
    ]
    to_x = [remote(p[4].at[1 - xl], p[5], ssem.at[XX + i], rsem.at[XX + i], beside) for i, p in enumerate(pieces)]
    to_last = [
        Ring(a, b, ssem.at[LAST + i], rsem.at[LAST + i], hz, NXH * NZ, lambda to: {"seq": to * NC + core})
        for i, (a, b) in enumerate(((fs, fr), (fsl, frl)))
    ]

    def after_core(i):
        sent, got, ys = pieces[i][:3]
        to_core[i].wait_recv()
        for n in range(NY):
            ys[n] = (sent[core, n].astype(F32) + got[n].astype(F32)).astype(BF16)
        to_y[i].start()

    def after_y(i):
        xs = pieces[i][4]
        to_y[i].recv()
        total = to_y[i].total()
        for h in range(NXL):
            xs[h] = (total[:, 384 * h : 384 * h + 384] if i == 1 else total[48 * h : 48 * h + 48]).astype(BF16)
        to_x[i].start()

    def after_x(i):
        xs, xr = pieces[i][4:]
        to_x[i].wait_recv()
        return (xs[xl].astype(F32) + xr[...].astype(F32)).astype(BF16)

    inward = {}
    for index, (name, source, target) in enumerate((
        ("x", x_hbm, x_ref), ("vw", vw_hbm, vw_ref), ("fb", fb_hbm, fb_ref), ("gw", gw_hbm, gw_ref), ("sb", sb_hbm, sb_ref),
        ("pm", pm_hbm, pm_ref), ("ex", ex_hbm, ex_ref), ("cot", cot_hbm, cot_ref), ("dn", dn_hbm, dn_ref),
        ("ow", ow_hbm, ow_ref), ("up", up_hbm, up_ref), ("p3", p3_hbm, p3_ref), ("p12", p12_hbm, p12_ref),
        ("fold", fold_hbm, fold_ref), ("ufold", ufold_hbm, ufold_ref),
    )):
        inward[name] = pltpu.make_async_copy(source, target, lsem.at[index])
        inward[name].start()
    outward = [pltpu.make_async_copy(out_ref, out_hbm, lsem.at[15])] + [
        pltpu.make_async_copy(
            gin_ref.at[pl.ds(HALF * ii, HALF)], gin_hbm.at[pl.ds(HALF * ii, HALF)], lsem.at[16 + ii]
        )
        for ii in range(2)
    ]

    def loaded(*names):
        for name in names:
            inward[name].wait()

    g1, g2 = g1_ref[...].reshape(1, D), g2_ref[...].reshape(1, D)

    def norm_first(rows, t):
        v = x_ref[rows, :].astype(F32)
        n1[rows, :] = (v * factor_of(v) * g1).astype(BF16)

    loaded("x")
    tiles(ROWS, 32, norm_first)
    loaded("vw", "fb")
    for n in range(NB):
        val[:, blk(n)] = dot(n1[:, blk(n)], vw_ref[:, blk(n)]).astype(BF16)
    for ct in range(3):
        lanes = lanes_of(ct)
        pair = [dot(fb_ref[ii], val[ii * HALF : (ii + 1) * HALF, lanes]) for ii in range(2)]
        s1[:, :, lanes] = pack_pair(*pair)
        if ct == 0:
            all_here()
        ex1[ct].start()

    loaded("sb", "pm", "ex")
    spread = dot(pm_ref[...], sb_ref[...]).astype(BF16)
    for ii in range(2):
        wide = dot(spread[ii * HALF : (ii + 1) * HALF], ex_ref[...])
        mm[ii] = jnp.where(same_block(wide.shape), wide, 0.0).astype(BF16)
    loaded("gw")
    for n in range(NB):
        gate[:, blk(n)] = dot(n1[:, blk(n)], gw_ref[:, blk(n)]).astype(BF16)
    loaded("cot", "dn")
    for n in range(NB):
        for ii in range(2):
            dact[ii, n] = dot(cot_ref[ii * HALF : (ii + 1) * HALF, blk(n)], dn_ref[:, blk(n)], 1, 1)

    for ct in range(3):
        ex1[ct].recv()
        lanes = lanes_of(ct)
        for ii in range(2):
            o = dot(mm[ii], r1[:, :, lanes].reshape(NS * 16, 256))
            s2[ii, :, :, 128 * ct : 128 * ct + 128] = pack_pair(o[:, :128], o[:, 128:])
            if ii == 0:
                ex2[0][ct].start()
    ex2[1][0].start()
    loaded("ow", "up")
    gain2[...] = jnp.zeros_like(gain2)

    def token_half(ii):
        base = ii * HALF
        half = slice(base, base + HALF)

        def rows_of(rows):
            return pl.ds(pl.multiple_of(base + rows.start, rows.size), rows.size)

        for part in ex2[ii]:
            part.recv()

        def gated(rows, t):
            part = r2[ii, pl.ds(pl.multiple_of(t * 4, 4), 4)]

            def store(lane, v):
                at = (rows_of(rows), slice(lane, lane + 128))
                mixed[at] = v.astype(BF16)
                y[at] = (v * gate[at].astype(F32)).astype(BF16)

            unpack_lanes(part, store)

        tiles(HALF, 32, gated)
        for n in range(NB):
            t768[:, blk(n)] = dot(y[half, blk(n)], ow_ref[:, blk(n)])

        def norm_second(rows, t):
            m = (x_ref[rows_of(rows), :].astype(F32) + t768[rows, :]).astype(BF16)
            mid[rows_of(rows), :] = m
            mf = m.astype(F32)
            n2[rows_of(rows), :] = (mf * factor_of(mf) * g2).astype(BF16)

        tiles(HALF, 32, norm_second)
        for n in range(NB):
            hbuf[...] = dot(n2[half, blk(n)], up_ref[:, blk(n, HB)])

            def gelu(rows, t):
                for lt in range(3):
                    lanes = slice(256 * lt, 256 * lt + 256)
                    wide = slice(n * HB + 256 * lt, n * HB + 256 * lt + 256)
                    value, slope = gelu_pair(hbuf[rows, lanes])
                    act[rows_of(rows), wide] = value.astype(BF16)
                    dpre[rows_of(rows), wide] = (slope * dact[ii, n, rows, lanes]).astype(BF16)

            tiles(HALF, 32, gelu)
            t768[:, blk(n)] = dot(dpre[half, blk(n, HB)], up_ref[:, blk(n, HB)], 1, 1)

        def norm_back_second(rows, t):
            mf = mid[rows_of(rows), :].astype(F32)
            f2 = factor_of(mf)
            u2 = mf * f2
            h2 = t768[rows, :]
            gain2[...] = fold_rows(h2 * u2, gain2[...])
            s = h2 * g2
            d = cot_ref[rows_of(rows), :].astype(F32) + f2 * (s - u2 * jnp.mean(s * u2, axis=-1, keepdims=True))
            dmid[rows_of(rows), :] = d.astype(BF16)

        tiles(HALF, 32, norm_back_second)
        for n in range(NB):
            t768[:, blk(n)] = dot(dmid[half, blk(n)], ow_ref[:, blk(n)], 1, 1)

        def gates_back(rows, t):
            dy = t768[rows, :]
            at = rows_of(rows)
            dgate[at, :] = (dy * mixed[at, :].astype(F32)).astype(BF16)
            dm = dy * gate[at, :].astype(F32)
            for ct in range(3):
                low, high = dm[:, 256 * ct : 256 * ct + 128], dm[:, 256 * ct + 128 : 256 * ct + 256]
                s3[ii, pl.ds(pl.multiple_of(t * 4, 4), 4), :, 128 * ct : 128 * ct + 128] = pack_pair(low, high)

        tiles(HALF, 32, gates_back)
        for part in ex3[ii]:
            part.start()

    token_half(0)
    token_half(1)

    loaded("p3", "p12")
    gain2_t = gain2[...].T
    inv_t = jnp.broadcast_to(1.0 / g1, (8, D)).T
    for n in range(NB):
        tmp[:, 0:D] = dot(cot_ref[:, blk(n)], act[:, blk(n, HB)], 0, 0).astype(BF16)
        tmp[:, D : D + DB] = dot(dgate[:, blk(n)], n1[:, blk(n)], 0, 0).astype(BF16)
        tmp[:, D + DB : GL] = dot(dmid[:, blk(n)], y[:, blk(n)], 0, 0).astype(BF16)
        tmp[:, GL:DL] = jnp.concatenate([gain2_t[blk(n)], jnp.zeros((DB, 120), F32)], axis=1).astype(BF16)
        moved = dot(p3_ref[...], tmp[...]).astype(BF16)
        cs_d[0, n] = moved[:96]
        cs_d[1, n] = moved[96:]
    to_core[0].start()

    def unpack_mixed(ii, ct):
        def step(rows, t):
            v = r3[ii, pl.ds(pl.multiple_of(t * 4, 4), 4), :, 128 * ct : 128 * ct + 128].astype(F32).reshape(4, 2, 8, 128)
            at = pl.ds(pl.multiple_of(ii * HALF + t * 32, 32), 32)
            for h in range(2):
                lane = 256 * ct + 128 * h
                dmu[at, lane : lane + 128] = v[:, h].reshape(32, 128).astype(BF16)

        tiles(HALF, 32, step)

    def second_back(ct):
        if ct == 0:
            ex3[0][0].recv()
            for every in range(3):
                unpack_mixed(0, every)
        ex3[1][ct].recv()
        unpack_mixed(1, ct)
        lanes = lanes_of(ct)
        s4[:, :, lanes] = dot(mm[...].reshape(ROWS, ROWS), dmu[:, lanes], 0, 0).astype(BF16).reshape(NS, 16, 256)
        ex4[ct].start()

    second_back(0)
    for n in range(NB):
        grad_up = dot(dpre[:, blk(n, HB)], n2[:, blk(n)], 0, 0).astype(BF16)
        for q in range(4):
            moved = dot(p12_ref[...], grad_up[blk(q)]).astype(BF16)
            cs_u[0, n, :, blk(q)] = moved[:96]
            cs_u[1, n, :, blk(q)] = moved[96:]
    to_core[1].start()
    second_back(1)
    after_core(0)
    second_back(2)
    after_core(1)

    for ii in range(2):
        g = dot(dmu[ii * HALF : (ii + 1) * HALF, :], r1[...].reshape(ROWS, D), 1, 1) * MIX_SCALE
        g = dot(jnp.where(same_block(g.shape), g, 0.0).astype(BF16), ex_ref[...], 1, 1)
        gsec[:, 64 * ii : 64 * ii + 64] = g.astype(BF16)
    for part in range(ND):
        gss[part] = gsec[32 * part : 32 * part + 32, :]
    gs_sum.start()

    for n in range(NB):
        t = dot(act[:, blk(n, HB)], dn_ref[:, blk(n)])
        out_ref[:, blk(n)] = (mid[:, blk(n)].astype(F32) + t).astype(BF16)
    outward[0].start()
    for n in range(NB):
        h1g[:, blk(n)] = dot(dgate[:, blk(n)], gw_ref[:, blk(n)], 1, 1)
        g = dot(n1[:, blk(n)], dgate[:, blk(n)], 0, 0) * gw_ref[:, blk(n)].astype(F32)
        gcol[blk(n), :] = jnp.broadcast_to(jnp.sum(g, axis=-1, keepdims=True), (DB, 8))
    gs_sum.recv()
    gsa[me_d] = gs_sum.total().astype(BF16)
    gs_all.start()
    after_y(0)
    after_y(1)

    for ct in range(3):
        ex4[ct].recv()
        lanes = lanes_of(ct)
        v = r4[:, :, lanes].astype(F32).reshape(NS, 2, 8, 256)
        for ii in range(2):
            half = slice(ii * HALF, (ii + 1) * HALF)
            df[half, lanes] = v[:, ii].reshape(HALF, 256).astype(BF16)
            g = dot(df[half, lanes], val[half, lanes], 1, 1)
            gfull[ii] = g if ct == 0 else gfull[ii] + g
            if ct == 2:
                for part in range(4):
                    gfs[4 * ii + part] = (gfull[ii, 64 * part : 64 * part + 64, :] * MIX_SCALE).astype(BF16)
        if ct == 2:
            gf_sum.start()
        for ii in range(2):
            half = slice(ii * HALF, (ii + 1) * HALF)
            dval[half, lanes] = dot(fb_ref[ii], df[half, lanes], 0, 0).astype(BF16)

    for n in range(NB):
        grad_v = dot(dval[:, blk(n)], n1[:, blk(n)], 0, 0)
        g = dot(n1[:, blk(n)], dval[:, blk(n)], 0, 0) * vw_ref[:, blk(n)].astype(F32)
        g = (jnp.sum(g, axis=-1, keepdims=True) + gcol[blk(n), 0:1]) * inv_t[blk(n), 0:1]
        column = jnp.where(lax.broadcasted_iota(jnp.int32, (DB, 64), 1) == 0, g, 0.0)
        moved = dot(p3_ref[...], jnp.concatenate([grad_v, column], axis=1).astype(BF16)).astype(BF16)
        cs_l[0, n] = moved[:96]
        cs_l[1, n] = moved[96:]
    to_core[2].start()

    loaded("fold", "ufold")
    dd, uu = after_x(0), after_x(1)
    folded = dot(fold_ref[:, 0:48], dd[:, 0:512]) + dot(fold_ref[:, 48:96], dd[:, 512:1024])
    fs[:, :, :] = folded.astype(BF16).reshape(16, 16, 512)
    tail = dot(fold_ref[:, 96:144], dd[:, 1024:1280]).astype(BF16).reshape(16, 16, 256)
    fs[:, :, 0:256] = fs[:, :, 0:256] + tail
    for h in range(NXH):
        u = uu[:, DB * h : DB * h + DB]
        low = dot(ufold_ref[:, 0:96], u).astype(BF16).reshape(8, 16, DB)
        high = dot(ufold_ref[:, 96:192], u).astype(BF16).reshape(8, 16, DB)
        at = slice(8 * h, 8 * h + 8)
        fs[at, :, 0:DB] = fs[at, :, 0:DB] + low
        fs[at, :, 256 : 256 + DB] = fs[at, :, 256 : 256 + DB] + high
    to_last[0].start()
    after_core(2)

    def input_gradient(ii):
        half = slice(ii * HALF, (ii + 1) * HALF)
        for n in range(NB):
            t768[:, blk(n)] = dot(dval[half, blk(n)], vw_ref[:, blk(n)], 1, 1)

        def norm_back_first(rows, t):
            at = pl.ds(pl.multiple_of(ii * HALF + t * 32, 32), 32)
            v = x_ref[at, :].astype(F32)
            f1 = factor_of(v)
            u1 = v * f1
            s = (t768[rows, :] + h1g[at, :]) * g1
            d = dmid[at, :].astype(F32) + f1 * (s - u1 * jnp.mean(s * u1, axis=-1, keepdims=True))
            gin_ref[at, :] = d.astype(BF16)

        tiles(HALF, 32, norm_back_first)
        outward[1 + ii].start()

    input_gradient(0)
    gf_sum.recv()
    gfa[me_d] = gf_sum.total().astype(BF16)
    gf_all.start()
    after_y(2)
    input_gradient(1)
    ll = after_x(2)
    folded = dot(fold_ref[:, 0:48], ll[:, 0:128]) + dot(fold_ref[:, 48:96], ll[:, 128:256])
    fsl[...] = folded.astype(BF16).reshape(16, 16, 128)
    to_last[1].start()

    to_last[0].recv()
    early_ref[...] = to_last[0].total()
    gs_all.recv()
    gf_all.recv()
    for part in range(ND):
        mix_ref[64 * part : 64 * part + 64, :] = gfa[part]
        mix_ref[512 + 16 * part : 528 + 16 * part, 0:128] = gsa[part, 0:16]
        mix_ref[512 + 16 * part : 528 + 16 * part, 128:256] = gsa[part, 16:32]
    to_last[1].recv()
    late_ref[...] = to_last[1].total()

    for part in ex1 + ex2[0] + ex2[1] + ex3[0] + ex3[1] + ex4 + [gs_sum, gs_all, gf_sum, gf_all] + to_y + to_last:
        part.sent()
    for copy in to_core + to_x:
        copy.wait_send()
    for copy in outward:
        copy.wait()


def finish_kernel(
    out_in, gin_in, mix_ref, early_ref, late_ref, pm_ref,
    out_ref, gin_ref, gv_ref, gg_ref, go_ref, gu_ref, gd_ref, g1_ref, g2_ref, gfirst_ref, gsecond_ref,
    spread, sem,
):
    copies = [pltpu.make_async_copy(out_in, out_ref, sem.at[0]), pltpu.make_async_copy(gin_in, gin_ref, sem.at[1])]
    for copy in copies:
        copy.start()
    for part in range(ND):
        at = 64 * (part % 4)
        gfirst_ref[part // 4, at : at + 64, :] = mix_ref[64 * part : 64 * part + 64, :].astype(F32)
        spread[32 * part : 32 * part + 16, :] = mix_ref[512 + 16 * part : 528 + 16 * part, 0:128]
        spread[32 * part + 16 : 32 * part + 32, :] = mix_ref[512 + 16 * part : 528 + 16 * part, 128:256]
    gsecond_ref[...] = dot(pm_ref[0:HALF, :], spread[:, 0:64], 0, 0) + dot(pm_ref[HALF:ROWS, :], spread[:, 64:128], 0, 0)
    total, late = early_ref[...] * ROW_SCALE, late_ref[...] * ROW_SCALE
    gd_ref[:, 0:512] = total[0:3]
    gd_ref[:, 512:768] = total[3:6, 0:256]
    gg_ref[...] = total[3:6, 256:448]
    go_ref[:, 0:64] = total[3:6, 448:512]
    go_ref[:, 64:192] = total[6:9, 0:128]
    gu_ref[0:6, :] = total[9:15, 0:192]
    gu_ref[6:12, :] = total[9:15, 256:448]
    gv_ref[:, 0:128] = late[0:3]
    gv_ref[:, 128:192] = late[3:6, 0:64]

    def across(column):
        square = lax.broadcasted_iota(jnp.int32, (8, 128), 0) == lax.broadcasted_iota(jnp.int32, (8, 128), 1)
        return jnp.sum(jnp.where(square, column, 0.0), axis=0, keepdims=True)[:, 0:3]

    pad = jnp.zeros((5, 1), F32)
    g2_ref[...] = across(jnp.concatenate([jnp.sum(total[6:9, 128:136], axis=1, keepdims=True), pad], axis=0))
    g1_ref[...] = across(jnp.concatenate([late[3:6, 64:65], pad], axis=0))
    for copy in copies:
        copy.wait()


def vmem_specs(count):
    return [pl.BlockSpec(memory_space=pltpu.VMEM)] * count


def any_specs(count):
    return [pl.BlockSpec(memory_space=pl.ANY)] * count


def body(inputs, cotangent, gain_first, gain_second, value_w, gate_w, out_w, up_w, down_w, first_blocks, second_blocks):
    perm_m, expand, perm3, perm12, fold, ufold = [jnp.asarray(a, BF16) for a in constants()]
    shape = jax.ShapeDtypeStruct
    vm = lambda *s: pltpu.VMEM(s, BF16)
    vf = lambda *s: pltpu.VMEM(s, F32)
    big = lambda: vm(ROWS, D)
    dma = pltpu.SemaphoreType.DMA
    out, gin, mix, early, late = pl.pallas_call(
        main_kernel,
        out_shape=[
            shape((ROWS, D), BF16), shape((ROWS, D), BF16), shape((640, 256), BF16), shape((16, 512), F32),
            shape((16, 128), F32),
        ],
        in_specs=any_specs(2) + vmem_specs(2) + any_specs(13),
        out_specs=any_specs(2) + vmem_specs(3),
        scratch_shapes=[
            big(), big(), vm(DB, D), vm(DB, D), vm(DB, D), vm(DB, NB * HB), vm(D, D), vm(2, 256, 256), vm(512, 64),
            vm(512, 512), vm(64, 512), vm(192, 192), vm(192, 192), vm(256, 144), vm(128, 192), big(), big(),
            big(), big(), big(), big(), big(), big(), big(), big(), big(), big(), big(),
            vm(ROWS, NB * HB), vm(ROWS, NB * HB), vf(2, NB, HALF, HB),
            vm(2, HALF, ROWS), big(), vf(HALF, D), vf(HALF, HB), vf(ROWS, D), vf(2, 256, 256),
            vm(NS, 16, D), vm(NS, 16, D), vm(2, NS, 16, 384), vm(2, NS, 16, 384),
            vm(2, NS, 16, 384), vm(2, NS, 16, 384), vm(NS, 16, D), vm(NS, 16, D),
            vm(ND, 32, 128), vm(ND, 32, 128), vm(ND, 32, 128), vm(ND, 64, 256), vm(ND, 64, 256), vm(ND, 64, 256),
            vm(HALF, 128), vf(8, D), vf(D, 8), vm(DB, DL),
            vm(2, NB, 96, DL), vm(2, NB, 96, UL), vm(2, NB, 96, LW), vm(NB, 96, DL), vm(NB, 96, UL), vm(NB, 96, LW),
            vm(NY, 96, DL), vm(NY, 96, UL), vm(NY, 96, LW), vm(NY, 96, DL), vm(NY, 96, UL), vm(NY, 96, LW),
            vm(2, 48, DL), vm(2, 96, 384), vm(2, 48, LW), vm(48, DL), vm(96, 384), vm(48, LW),
            vm(16, 16, 512), vm(16, 16, 512), vm(16, 16, 128), vm(16, 16, 128),
            dma((SEMS,)), dma((SEMS,)), dma((18,)),
        ],
        compiler_params=pltpu.CompilerParams(
            collective_id=0, has_side_effects=True, vmem_limit_bytes=VMEM_LIMIT
        ),
    )(
        inputs.reshape(ROWS, D), cotangent.reshape(ROWS, D), gain_first, gain_second,
        value_w, gate_w, out_w, up_w, down_w, first_blocks, second_blocks.reshape(512, 64),
        perm_m, expand, perm3, perm12, fold, ufold,
    )
    out, gin, gv, gg, go, gu, gd, g1, g2, gfirst, gsecond = pl.pallas_call(
        finish_kernel,
        out_shape=[
            shape((ROWS, D), BF16), shape((ROWS, D), BF16), shape((3, DB), F32), shape((3, DB), F32), shape((3, DB), F32),
            shape((12, DB), F32), shape((3, HB), F32), shape((1, 3), F32), shape((1, 3), F32), shape((2, 256, 256), F32),
            shape((512, 64), F32),
        ],
        in_specs=any_specs(2) + vmem_specs(4),
        out_specs=vmem_specs(11),
        scratch_shapes=[vm(HALF, 128), dma((2,))],
    )(out, gin, mix, early, late, perm_m)
    return (
        out.reshape(1, ROWS, D), gin.reshape(1, ROWS, D), gv.T, gg.T, go.T, gu.T, gd.T, g1.reshape(3), g2.reshape(3),
        gfirst, gsecond.reshape(8, 64, 64),
    )


def solution(mesh):
    tokens, whole = P("dp", "seq", None), P("seq", None, None)
    columns = P(None, ("dp", "seq"))
    gains = P(("dp", "seq"))
    return jax.shard_map(
        body,
        mesh=mesh,
        in_specs=(tokens, tokens, P(), P(), P(), P(), P(), P(), P(), whole, whole),
        out_specs=(tokens, tokens, columns, columns, columns, columns, columns, gains, gains, whole, whole),
        check_vma=False,
    )
```

time: 178 us -> 122 us (0.69)
  Pallas kernels: 162 us -> 119 us
  local copies, waits for them, and re-layouts: 15 us -> 0 us
    pallas_call x1, Pallas kernels: 53.1 us -> 4 us  [body(): pl.pallas_call(finish_kernel, out_shape=[shape((ROWS, D), BF16), shape((R...]
    unnamed x23 -> x0, local copies, waits for them, and re-layouts: 12.4 us -> none
    pallas_call x1, Pallas kernels: 109 us -> 115 us  [body(): pl.pallas_call(main_kernel, out_shape=[shape((ROWS, D), BF16), shape((ROW...]
    reshape x2 -> x0, local copies, waits for them, and re-layouts: 2.53 us -> none  [the longest x1 1.27 us: body(): gain_first.reshape(1, D)]
where the time goes in v2:
time: 122 us; the launch traced here: 120 us
  Pallas kernels  119 us (98%)
    pallas_call x1, Pallas kernels, body(): pl.pallas_call(main_kernel, out_shape=[shape((ROWS, D), BF16), shape((ROW...  115 us
    pallas_call x1, Pallas kernels, body(): pl.pallas_call(finish_kernel, out_shape=[shape((ROWS, D), BF16), shape((R...  4 us

profile of v2, /device:TPU:1, one launch (start us, length us, event | category | flops | bytes accessed | tf_op | source)
XLA Modules:
  0.0 120.3 jit_solution(14859413268015975305)
XLA Ops:
  0.6 115.5 %shard_map.248 = (bf16[512,768]{1,0:T(8,128)(2,1)}, bf16[512,768]{1,0:T(8,128)(2,1)}, bf16[640,256]{1,0:T(8,128)(2,1)}, f32[16,512]{1,0:T(8,128)}, f32[16,128]{1,0:T(8,128)}) custom-call(bf16[512,768]{1,0:T(8,128)(2,1)} %bitcast.13, bf16[512,768]{1,0:T(8,128)(2,1)} %bitcast.14, f32[768]{0:T(1024)} %g1_ref.1, f32[768]{0:T(1024)} %g2_ref.1, ...), custom_call_target="tpu_custom_call" | custom-call | tf_op jit(solution)/shard_map/pallas_call | solution.py:636
  116.1 4.0 %shard_map.249 = (bf16[512,768]{1,0:T(8,128)(2,1)}, bf16[512,768]{1,0:T(8,128)(2,1)}, f32[3,192]{1,0:T(4,128)}, f32[3,192]{1,0:T(4,128)}, f32[3,192]{1,0:T(4,128...) custom-call(bf16[512,768]{1,0:T(8,128)(2,1)} %get-tuple-element.27.o, ...), custom_call_target="tpu_custom_call" | custom-call | tf_op jit(solution)/shard_map/pallas_call | solution.py:668

commit v3 on v2

--- a/solution.py
+++ b/solution.py
@@ -18,10 +18,9 @@
 D, NB, DB, HB, ROWS, HALF = 768, 4, 192, 768, 512, 256
 ROW_SCALE = 1.0 / math.sqrt(131072.0)
 MIX_SCALE = 1.0 / math.sqrt(6144.0)
-DL, UL, LW = 1280, 768, 256
-GL = 1152
-A1, A2, A2B, A3, A3B, A4, GS, GF, CORE, YY, XX, LAST = 0, 3, 6, 7, 8, 11, 14, 16, 18, 21, 24, 27
-SEMS = 29
+DL, UL, LW = 1152, 768, 256
+A1, A2, A2B, A3, A3B, A4, GS, GF, CORE, YY, XX, LAST = 0, 3, 6, 7, 8, 11, 15, 17, 21, 33, 36, 38
+SEMS = 40
 VMEM_LIMIT = 60 * 2**20
 
 
@@ -129,6 +128,12 @@
         self.sbuf, self.rbuf, self.sems = sbuf, rbuf, (ssem, rsem)
         self.me, self.count, self.device, self.same = me, count, device, same
 
+    def one(self, to):
+        remote(self.sbuf.at[to], self.rbuf.at[self.me], *self.sems, self.device(to)).start()
+
+    def own(self, to):
+        self.rbuf[to] = self.sbuf[to]
+
     def start(self):
         def send(k, carry):
             to = lax.rem(self.me + k, self.count)
@@ -185,12 +190,6 @@
 
 def factor_of(rows):
     return lax.rsqrt(jnp.mean(rows * rows, axis=-1, keepdims=True) + EPS)
-
-
-def fold_rows(product, acc):
-    for r in range(product.shape[0] // 8):
-        acc = acc + product[8 * r : 8 * r + 8]
-    return acc
 
 
 def gelu_pair(h):
@@ -217,10 +216,10 @@
     out_hbm, gin_hbm, mix_ref, early_ref, late_ref,
     x_ref, cot_ref, vw_ref, gw_ref, ow_ref, up_ref, dn_ref, fb_ref, sb_ref,
     pm_ref, ex_ref, p3_ref, p12_ref, fold_ref, ufold_ref, out_ref, gin_ref,
-    n1, val, gate, mixed, y, mid, n2, dmid, dgate, df, dval, act, dpre, dact, mm, dmu, t768, hbuf, h1g, gfull,
-    s1, r1, s2, r2, s3, r3, s4, r4, gss, gsr, gsa, gfs, gfr, gfa, gsec, gain2, gcol, tmp,
+    n1, val, gate, mixed, y, mid, n2, dmid, dgate, df, dval, act, dpre, dact, mm, dmu, t768, hbuf, h1g,
+    s1, r1, s2, r2, s3, r3, s4, r4, gss, gsr, gsa, gfs, gfr, gfa, gsec, gcol, gcol2, tmp,
     cs_d, cs_u, cs_l, cr_d, cr_u, cr_l, ys_d, ys_u, ys_l, yr_d, yr_u, yr_l,
-    xs_d, xs_u, xs_l, xr_d, xr_u, xr_l, fs, fr, fsl, frl,
+    xs_d, xs_u, xr_d, xr_u, fs, fr, fsl, frl,
     ssem, rsem, lsem,
 ):
     me_s, me_d = lax.axis_index("seq"), lax.axis_index("dp")
@@ -243,32 +242,52 @@
         [exchange(s3.at[0], r3.at[0], A3)],
         [exchange(s3.at[1], r3.at[1], A3B + ct, lanes_of(ct, 128)) for ct in range(3)],
     ]
-    ex4 = [exchange(s4, r4, A4 + ct, lanes_of(ct)) for ct in range(3)]
+    ex4 = [exchange(s4.at[0], r4.at[0], A4 + ct, lanes_of(ct, 128)) for ct in range(3)] + [exchange(s4.at[1], r4.at[1], A4 + 3)]
 
     def over_dp(sbuf, rbuf, index, same=False):
         return Ring(sbuf, rbuf, ssem.at[index], rsem.at[index], me_d, ND, lambda to: {"dp": to}, same)
 
     gs_sum, gs_all = over_dp(gss, gsr, GS), over_dp(gsa, gsa, GS + 1, True)
-    gf_sum, gf_all = over_dp(gfs, gfr, GF), over_dp(gfa, gfa, GF + 1, True)
-    pieces = ((cs_d, cr_d, ys_d, yr_d, xs_d, xr_d), (cs_u, cr_u, ys_u, yr_u, xs_u, xr_u), (cs_l, cr_l, ys_l, yr_l, xs_l, xr_l))
+    gf_sum = [over_dp(gfs.at[ii], gfr.at[ii], GF + ii) for ii in range(2)]
+    gf_all = [over_dp(gfa.at[ii], gfa.at[ii], GF + 2 + ii, True) for ii in range(2)]
+    pieces = ((cs_d, cr_d, ys_d, yr_d, xs_d, xr_d), (cs_u, cr_u, ys_u, yr_u, xs_u, xr_u), (cs_l, cr_l, ys_l, yr_l))
     mate, beside = {"seq": hz * NC + 1 - core}, {"dp": yy * NXL + 1 - xl}
-    to_core = [remote(p[0].at[1 - core], p[1], ssem.at[CORE + i], rsem.at[CORE + i], mate) for i, p in enumerate(pieces)]
+    to_core = [
+        [
+            remote(p[0].at[1 - core, n], p[1].at[n], ssem.at[CORE + 4 * i + n], rsem.at[CORE + 4 * i + n], mate)
+            for n in range(NY)
+        ]
+        for i, p in enumerate(pieces)
+    ]
     to_y = [
         Ring(p[2], p[3], ssem.at[YY + i], rsem.at[YY + i], yy, NY, lambda to: {"dp": to * NXL + xl})
-        for i, p in enumerate(pieces)
-    ]
-    to_x = [remote(p[4].at[1 - xl], p[5], ssem.at[XX + i], rsem.at[XX + i], beside) for i, p in enumerate(pieces)]
+        for i, p in enumerate(pieces[:2])
+    ] + [over_dp(ys_l, yr_l, YY + 2)]
+    to_x = [remote(p[4].at[1 - xl], p[5], ssem.at[XX + i], rsem.at[XX + i], beside) for i, p in enumerate(pieces[:2])]
     to_last = [
         Ring(a, b, ssem.at[LAST + i], rsem.at[LAST + i], hz, NXH * NZ, lambda to: {"seq": to * NC + core})
         for i, (a, b) in enumerate(((fs, fr), (fsl, frl)))
     ]
 
-    def after_core(i):
+    def after_core(i, n):
         sent, got, ys = pieces[i][:3]
-        to_core[i].wait_recv()
-        for n in range(NY):
-            ys[n] = (sent[core, n].astype(F32) + got[n].astype(F32)).astype(BF16)
-        to_y[i].start()
+        to_core[i][n].wait_recv()
+        both = (sent[core, n].astype(F32) + got[n].astype(F32)).astype(BF16)
+        if i == 2:
+            for h in range(NXL):
+                ys[NXL * n + h] = both[48 * h : 48 * h + 48]
+            if n == NY - 1:
+                to_y[2].start()
+        else:
+            ys[n] = both
+
+            @pl.when(yy != n)
+            def _():
+                to_y[i].one(n)
+
+            @pl.when(yy == n)
+            def _():
+                to_y[i].own(n)
 
     def after_y(i):
         xs = pieces[i][4]
@@ -312,9 +331,9 @@
     loaded("x")
     tiles(ROWS, 32, norm_first)
     loaded("vw", "fb")
-    for n in range(NB):
-        val[:, blk(n)] = dot(n1[:, blk(n)], vw_ref[:, blk(n)]).astype(BF16)
     for ct in range(3):
+        for n in ((0, 1), (2,), (3,))[ct]:
+            val[:, blk(n)] = dot(n1[:, blk(n)], vw_ref[:, blk(n)]).astype(BF16)
         lanes = lanes_of(ct)
         pair = [dot(fb_ref[ii], val[ii * HALF : (ii + 1) * HALF, lanes]) for ii in range(2)]
         s1[:, :, lanes] = pack_pair(*pair)
@@ -345,7 +364,6 @@
                 ex2[0][ct].start()
     ex2[1][0].start()
     loaded("ow", "up")
-    gain2[...] = jnp.zeros_like(gain2)
 
     def token_half(ii):
         base = ii * HALF
@@ -397,7 +415,6 @@
             f2 = factor_of(mf)
             u2 = mf * f2
             h2 = t768[rows, :]
-            gain2[...] = fold_rows(h2 * u2, gain2[...])
             s = h2 * g2
             d = cot_ref[rows_of(rows), :].astype(F32) + f2 * (s - u2 * jnp.mean(s * u2, axis=-1, keepdims=True))
             dmid[rows_of(rows), :] = d.astype(BF16)
@@ -422,19 +439,6 @@
     token_half(0)
     token_half(1)
 
-    loaded("p3", "p12")
-    gain2_t = gain2[...].T
-    inv_t = jnp.broadcast_to(1.0 / g1, (8, D)).T
-    for n in range(NB):
-        tmp[:, 0:D] = dot(cot_ref[:, blk(n)], act[:, blk(n, HB)], 0, 0).astype(BF16)
-        tmp[:, D : D + DB] = dot(dgate[:, blk(n)], n1[:, blk(n)], 0, 0).astype(BF16)
-        tmp[:, D + DB : GL] = dot(dmid[:, blk(n)], y[:, blk(n)], 0, 0).astype(BF16)
-        tmp[:, GL:DL] = jnp.concatenate([gain2_t[blk(n)], jnp.zeros((DB, 120), F32)], axis=1).astype(BF16)
-        moved = dot(p3_ref[...], tmp[...]).astype(BF16)
-        cs_d[0, n] = moved[:96]
-        cs_d[1, n] = moved[96:]
-    to_core[0].start()
-
     def unpack_mixed(ii, ct):
         def step(rows, t):
             v = r3[ii, pl.ds(pl.multiple_of(t * 4, 4), 4), :, 128 * ct : 128 * ct + 128].astype(F32).reshape(4, 2, 8, 128)
@@ -453,21 +457,56 @@
         ex3[1][ct].recv()
         unpack_mixed(1, ct)
         lanes = lanes_of(ct)
-        s4[:, :, lanes] = dot(mm[...].reshape(ROWS, ROWS), dmu[:, lanes], 0, 0).astype(BF16).reshape(NS, 16, 256)
+        o = dot(mm[...].reshape(ROWS, ROWS), dmu[:, lanes], 0, 0).reshape(NS, 2, 8, 256)
+        for ii in range(2):
+            low, high = o[:, ii, :, :128].reshape(HALF, 128), o[:, ii, :, 128:].reshape(HALF, 128)
+            s4[ii, :, :, 128 * ct : 128 * ct + 128] = pack_pair(low, high)
         ex4[ct].start()
-
-    second_back(0)
-    for n in range(NB):
-        grad_up = dot(dpre[:, blk(n, HB)], n2[:, blk(n)], 0, 0).astype(BF16)
+        if ct == 2:
+            ex4[3].start()
+
+    loaded("p3", "p12")
+    inv1 = jnp.broadcast_to(1.0 / g1, (8, D)).T
+    inv2 = jnp.broadcast_to(1.0 / g2, (8, D)).T
+
+    def piece_down(n):
+        tmp[:, 0:D] = dot(cot_ref[:, blk(n)], act[:, blk(n, HB)], 0, 0).astype(BF16)
+        tmp[:, D : D + DB] = dot(dgate[:, blk(n)], n1[:, blk(n)], 0, 0).astype(BF16)
+        tmp[:, D + DB : DL] = dot(dmid[:, blk(n)], y[:, blk(n)], 0, 0).astype(BF16)
+        moved = dot(p3_ref[...], tmp[...]).astype(BF16)
+        cs_d[0, n] = moved[:96]
+        cs_d[1, n] = moved[96:]
+        to_core[0][n].start()
+
+    def piece_up(n):
+        g = dot(n2[:, blk(n)], dpre[:, blk(n, HB)], 0, 0)
+        column = jnp.sum(g * up_ref[:, blk(n, HB)].astype(F32), axis=-1, keepdims=True) * inv2[blk(n), 0:1]
+        gcol2[blk(n), :] = jnp.broadcast_to(column, (DB, 8))
         for q in range(4):
-            moved = dot(p12_ref[...], grad_up[blk(q)]).astype(BF16)
+            moved = dot(p12_ref[...], g[:, blk(q)].astype(BF16), 1, 1).astype(BF16)
             cs_u[0, n, :, blk(q)] = moved[:96]
             cs_u[1, n, :, blk(q)] = moved[96:]
-    to_core[1].start()
+        to_core[1][n].start()
+
+    piece_down(0)
+    piece_down(1)
+    after_core(0, 0)
+    piece_down(2)
+    after_core(0, 1)
+    piece_down(3)
+    after_core(0, 2)
+    second_back(0)
+    piece_up(0)
+    after_core(0, 3)
+    piece_up(1)
+    after_core(1, 0)
     second_back(1)
-    after_core(0)
+    piece_up(2)
+    after_core(1, 1)
+    piece_up(3)
+    after_core(1, 2)
     second_back(2)
-    after_core(1)
+    after_core(1, 3)
 
     for ii in range(2):
         g = dot(dmu[ii * HALF : (ii + 1) * HALF, :], r1[...].reshape(ROWS, D), 1, 1) * MIX_SCALE
@@ -481,6 +520,7 @@
         t = dot(act[:, blk(n, HB)], dn_ref[:, blk(n)])
         out_ref[:, blk(n)] = (mid[:, blk(n)].astype(F32) + t).astype(BF16)
     outward[0].start()
+    after_y(0)
     for n in range(NB):
         h1g[:, blk(n)] = dot(dgate[:, blk(n)], gw_ref[:, blk(n)], 1, 1)
         g = dot(n1[:, blk(n)], dgate[:, blk(n)], 0, 0) * gw_ref[:, blk(n)].astype(F32)
@@ -488,43 +528,73 @@
     gs_sum.recv()
     gsa[me_d] = gs_sum.total().astype(BF16)
     gs_all.start()
-    after_y(0)
-    after_y(1)
-
+
+    def block_back(ii):
+        half = slice(ii * HALF, (ii + 1) * HALF)
+
+        def unpack(rows, t):
+            def store(lane, v):
+                df[pl.ds(pl.multiple_of(ii * HALF + t * 32, 32), 32), lane : lane + 128] = v.astype(BF16)
+
+            unpack_lanes(r4[ii, pl.ds(pl.multiple_of(t * 4, 4), 4)], store)
+
+        tiles(HALF, 32, unpack)
+        g = (dot(df[half, :], val[half, :], 1, 1) * MIX_SCALE).astype(BF16)
+        for part in range(ND):
+            gfs[ii, part] = g[32 * part : 32 * part + 32]
+        gf_sum[ii].start()
+        dval[half, :] = dot(fb_ref[ii], df[half, :], 0, 0).astype(BF16)
+
+    def input_gradient(ii):
+        half = slice(ii * HALF, (ii + 1) * HALF)
+        for n in range(NB):
+            t768[:, blk(n)] = dot(dval[half, blk(n)], vw_ref[:, blk(n)], 1, 1)
+
+        def norm_back_first(rows, t):
+            at = pl.ds(pl.multiple_of(ii * HALF + t * 32, 32), 32)
+            v = x_ref[at, :].astype(F32)
+            f1 = factor_of(v)
+            u1 = v * f1
+            s = (t768[rows, :] + h1g[at, :]) * g1
+            d = dmid[at, :].astype(F32) + f1 * (s - u1 * jnp.mean(s * u1, axis=-1, keepdims=True))
+            gin_ref[at, :] = d.astype(BF16)
+
+        tiles(HALF, 32, norm_back_first)
+        outward[1 + ii].start()
+
+    def share_mixing(ii):
+        gf_sum[ii].recv()
+        gfa[ii, me_d] = gf_sum[ii].total().astype(BF16)
+        gf_all[ii].start()
+
+    loaded("fold", "ufold")
     for ct in range(3):
         ex4[ct].recv()
-        lanes = lanes_of(ct)
-        v = r4[:, :, lanes].astype(F32).reshape(NS, 2, 8, 256)
-        for ii in range(2):
-            half = slice(ii * HALF, (ii + 1) * HALF)
-            df[half, lanes] = v[:, ii].reshape(HALF, 256).astype(BF16)
-            g = dot(df[half, lanes], val[half, lanes], 1, 1)
-            gfull[ii] = g if ct == 0 else gfull[ii] + g
-            if ct == 2:
-                for part in range(4):
-                    gfs[4 * ii + part] = (gfull[ii, 64 * part : 64 * part + 64, :] * MIX_SCALE).astype(BF16)
-        if ct == 2:
-            gf_sum.start()
-        for ii in range(2):
-            half = slice(ii * HALF, (ii + 1) * HALF)
-            dval[half, lanes] = dot(fb_ref[ii], df[half, lanes], 0, 0).astype(BF16)
-
+    block_back(0)
+    input_gradient(0)
+    after_y(1)
+    share_mixing(0)
+    ex4[3].recv()
+    block_back(1)
+
+    place = lax.broadcasted_iota(jnp.int32, (DB, 64), 1)
     for n in range(NB):
-        grad_v = dot(dval[:, blk(n)], n1[:, blk(n)], 0, 0)
-        g = dot(n1[:, blk(n)], dval[:, blk(n)], 0, 0) * vw_ref[:, blk(n)].astype(F32)
-        g = (jnp.sum(g, axis=-1, keepdims=True) + gcol[blk(n), 0:1]) * inv_t[blk(n), 0:1]
-        column = jnp.where(lax.broadcasted_iota(jnp.int32, (DB, 64), 1) == 0, g, 0.0)
-        moved = dot(p3_ref[...], jnp.concatenate([grad_v, column], axis=1).astype(BF16)).astype(BF16)
+        g = dot(n1[:, blk(n)], dval[:, blk(n)], 0, 0)
+        first = jnp.sum(g * vw_ref[:, blk(n)].astype(F32), axis=-1, keepdims=True) + gcol[blk(n), 0:1]
+        columns = jnp.where(place == 0, first * inv1[blk(n), 0:1], jnp.where(place == 1, gcol2[blk(n), 0:1], 0.0))
+        grad_v = dot(p3_ref[...], g.astype(BF16), 1, 1).astype(BF16)
+        gains = dot(p3_ref[...], columns.astype(BF16)).astype(BF16)
+        moved = jnp.concatenate([grad_v, gains], axis=1)
         cs_l[0, n] = moved[:96]
         cs_l[1, n] = moved[96:]
-    to_core[2].start()
-
-    loaded("fold", "ufold")
+        to_core[2][n].start()
+    for n in range(NB):
+        after_core(2, n)
     dd, uu = after_x(0), after_x(1)
     folded = dot(fold_ref[:, 0:48], dd[:, 0:512]) + dot(fold_ref[:, 48:96], dd[:, 512:1024])
     fs[:, :, :] = folded.astype(BF16).reshape(16, 16, 512)
-    tail = dot(fold_ref[:, 96:144], dd[:, 1024:1280]).astype(BF16).reshape(16, 16, 256)
-    fs[:, :, 0:256] = fs[:, :, 0:256] + tail
+    tail = dot(fold_ref[:, 96:144], dd[:, 1024:1152]).astype(BF16).reshape(16, 16, 128)
+    fs[:, :, 0:128] = fs[:, :, 0:128] + tail
     for h in range(NXH):
         u = uu[:, DB * h : DB * h + DB]
         low = dot(ufold_ref[:, 0:96], u).astype(BF16).reshape(8, 16, DB)
@@ -533,32 +603,10 @@
         fs[at, :, 0:DB] = fs[at, :, 0:DB] + low
         fs[at, :, 256 : 256 + DB] = fs[at, :, 256 : 256 + DB] + high
     to_last[0].start()
-    after_core(2)
-
-    def input_gradient(ii):
-        half = slice(ii * HALF, (ii + 1) * HALF)
-        for n in range(NB):
-            t768[:, blk(n)] = dot(dval[half, blk(n)], vw_ref[:, blk(n)], 1, 1)
-
-        def norm_back_first(rows, t):
-            at = pl.ds(pl.multiple_of(ii * HALF + t * 32, 32), 32)
-            v = x_ref[at, :].astype(F32)
-            f1 = factor_of(v)
-            u1 = v * f1
-            s = (t768[rows, :] + h1g[at, :]) * g1
-            d = dmid[at, :].astype(F32) + f1 * (s - u1 * jnp.mean(s * u1, axis=-1, keepdims=True))
-            gin_ref[at, :] = d.astype(BF16)
-
-        tiles(HALF, 32, norm_back_first)
-        outward[1 + ii].start()
-
-    input_gradient(0)
-    gf_sum.recv()
-    gfa[me_d] = gf_sum.total().astype(BF16)
-    gf_all.start()
-    after_y(2)
+    share_mixing(1)
     input_gradient(1)
-    ll = after_x(2)
+    to_y[2].recv()
+    ll = to_y[2].total().astype(BF16)
     folded = dot(fold_ref[:, 0:48], ll[:, 0:128]) + dot(fold_ref[:, 48:96], ll[:, 128:256])
     fsl[...] = folded.astype(BF16).reshape(16, 16, 128)
     to_last[1].start()
@@ -566,17 +614,19 @@
     to_last[0].recv()
     early_ref[...] = to_last[0].total()
     gs_all.recv()
-    gf_all.recv()
+    for part in gf_all:
+        part.recv()
     for part in range(ND):
-        mix_ref[64 * part : 64 * part + 64, :] = gfa[part]
+        for ii in range(2):
+            mix_ref[HALF * ii + 32 * part : HALF * ii + 32 * part + 32, :] = gfa[ii, part]
         mix_ref[512 + 16 * part : 528 + 16 * part, 0:128] = gsa[part, 0:16]
         mix_ref[512 + 16 * part : 528 + 16 * part, 128:256] = gsa[part, 16:32]
     to_last[1].recv()
     late_ref[...] = to_last[1].total()
 
-    for part in ex1 + ex2[0] + ex2[1] + ex3[0] + ex3[1] + ex4 + [gs_sum, gs_all, gf_sum, gf_all] + to_y + to_last:
+    for part in ex1 + ex2[0] + ex2[1] + ex3[0] + ex3[1] + ex4 + [gs_sum, gs_all] + gf_sum + gf_all + to_y + to_last:
         part.sent()
-    for copy in to_core + to_x:
+    for copy in to_core[0] + to_core[1] + to_core[2] + to_x:
         copy.wait_send()
     for copy in outward:
         copy.wait()
@@ -584,15 +634,24 @@
 
 def finish_kernel(
     out_in, gin_in, mix_ref, early_ref, late_ref, pm_ref,
-    out_ref, gin_ref, gv_ref, gg_ref, go_ref, gu_ref, gd_ref, g1_ref, g2_ref, gfirst_ref, gsecond_ref,
-    spread, sem,
+    out_hbm, gin_hbm, gv_ref, gg_ref, go_ref, gu_ref, gd_ref, g1_ref, g2_ref, gfirst_ref, gsecond_ref,
+    spread, out_v, gin_v, sem,
 ):
-    copies = [pltpu.make_async_copy(out_in, out_ref, sem.at[0]), pltpu.make_async_copy(gin_in, gin_ref, sem.at[1])]
-    for copy in copies:
+    parts = [
+        (a.at[pl.ds(128 * q, 128)], v.at[pl.ds(128 * q, 128)], b.at[pl.ds(128 * q, 128)])
+        for q in range(4)
+        for a, v, b in ((out_in, out_v, out_hbm), (gin_in, gin_v, gin_hbm))
+    ]
+    inward = [pltpu.make_async_copy(a, v, sem.at[k]) for k, (a, v, b) in enumerate(parts)]
+    outward = [pltpu.make_async_copy(v, b, sem.at[8 + k]) for k, (a, v, b) in enumerate(parts)]
+    for copy in inward:
         copy.start()
+    for here, there in zip(inward, outward):
+        here.wait()
+        there.start()
+    for ii in range(2):
+        gfirst_ref[ii] = mix_ref[HALF * ii : HALF * ii + HALF, :].astype(F32)
     for part in range(ND):
-        at = 64 * (part % 4)
-        gfirst_ref[part // 4, at : at + 64, :] = mix_ref[64 * part : 64 * part + 64, :].astype(F32)
         spread[32 * part : 32 * part + 16, :] = mix_ref[512 + 16 * part : 528 + 16 * part, 0:128]
         spread[32 * part + 16 : 32 * part + 32, :] = mix_ref[512 + 16 * part : 528 + 16 * part, 128:256]
     gsecond_ref[...] = dot(pm_ref[0:HALF, :], spread[:, 0:64], 0, 0) + dot(pm_ref[HALF:ROWS, :], spread[:, 64:128], 0, 0)
@@ -612,9 +671,9 @@
         return jnp.sum(jnp.where(square, column, 0.0), axis=0, keepdims=True)[:, 0:3]
 
     pad = jnp.zeros((5, 1), F32)
-    g2_ref[...] = across(jnp.concatenate([jnp.sum(total[6:9, 128:136], axis=1, keepdims=True), pad], axis=0))
+    g2_ref[...] = across(jnp.concatenate([late[3:6, 65:66], pad], axis=0))
     g1_ref[...] = across(jnp.concatenate([late[3:6, 64:65], pad], axis=0))
-    for copy in copies:
+    for copy in outward:
         copy.wait()
 
 
@@ -646,14 +705,14 @@
             vm(512, 512), vm(64, 512), vm(192, 192), vm(192, 192), vm(256, 144), vm(128, 192), big(), big(),
             big(), big(), big(), big(), big(), big(), big(), big(), big(), big(), big(),
             vm(ROWS, NB * HB), vm(ROWS, NB * HB), vf(2, NB, HALF, HB),
-            vm(2, HALF, ROWS), big(), vf(HALF, D), vf(HALF, HB), vf(ROWS, D), vf(2, 256, 256),
+            vm(2, HALF, ROWS), big(), vf(HALF, D), vf(HALF, HB), vf(ROWS, D),
             vm(NS, 16, D), vm(NS, 16, D), vm(2, NS, 16, 384), vm(2, NS, 16, 384),
-            vm(2, NS, 16, 384), vm(2, NS, 16, 384), vm(NS, 16, D), vm(NS, 16, D),
-            vm(ND, 32, 128), vm(ND, 32, 128), vm(ND, 32, 128), vm(ND, 64, 256), vm(ND, 64, 256), vm(ND, 64, 256),
-            vm(HALF, 128), vf(8, D), vf(D, 8), vm(DB, DL),
+            vm(2, NS, 16, 384), vm(2, NS, 16, 384), vm(2, NS, 16, 384), vm(2, NS, 16, 384),
+            vm(ND, 32, 128), vm(ND, 32, 128), vm(ND, 32, 128), vm(2, ND, 32, 256), vm(2, ND, 32, 256), vm(2, ND, 32, 256),
+            vm(HALF, 128), vf(D, 8), vf(D, 8), vm(DB, DL),
             vm(2, NB, 96, DL), vm(2, NB, 96, UL), vm(2, NB, 96, LW), vm(NB, 96, DL), vm(NB, 96, UL), vm(NB, 96, LW),
-            vm(NY, 96, DL), vm(NY, 96, UL), vm(NY, 96, LW), vm(NY, 96, DL), vm(NY, 96, UL), vm(NY, 96, LW),
-            vm(2, 48, DL), vm(2, 96, 384), vm(2, 48, LW), vm(48, DL), vm(96, 384), vm(48, LW),
+            vm(NY, 96, DL), vm(NY, 96, UL), vm(ND, 48, LW), vm(NY, 96, DL), vm(NY, 96, UL), vm(ND, 48, LW),
+            vm(2, 48, DL), vm(2, 96, 384), vm(48, DL), vm(96, 384),
             vm(16, 16, 512), vm(16, 16, 512), vm(16, 16, 128), vm(16, 16, 128),
             dma((SEMS,)), dma((SEMS,)), dma((18,)),
         ],
@@ -673,8 +732,8 @@
             shape((512, 64), F32),
         ],
         in_specs=any_specs(2) + vmem_specs(4),
-        out_specs=vmem_specs(11),
-        scratch_shapes=[vm(HALF, 128), dma((2,))],
+        out_specs=any_specs(2) + vmem_specs(9),
+        scratch_shapes=[vm(HALF, 128), big(), big(), dma((16,))],
     )(out, gin, mix, early, late, perm_m)
     return (
         out.reshape(1, ROWS, D), gin.reshape(1, ROWS, D), gv.T, gg.T, go.T, gu.T, gd.T, g1.reshape(3), g2.reshape(3),

time: 122 us -> 119 us (0.975); the launches traced: 120 us -> 119 us
    pallas_call x1, Pallas kernels: 115 us -> 113 us  [body(): pl.pallas_call(main_kernel, out_shape=[shape((ROWS, D), BF16), shape((ROW...]
where the time goes in v3:
time: 119 us
  Pallas kernels  118 us (99%)
    pallas_call x1, Pallas kernels, body(): pl.pallas_call(main_kernel, out_shape=[shape((ROWS, D), BF16), shape((ROW...  113 us
    pallas_call x1, Pallas kernels, body(): pl.pallas_call(finish_kernel, out_shape=[shape((ROWS, D), BF16), shape((R...  4.38 us

profile of v3, /device:TPU:1, one launch (start us, length us, event | category | flops | bytes accessed | tf_op | source)
XLA Modules:
  0.0 118.7 jit_solution(8521968802362028011)
XLA Ops:
  0.6 113.5 %shard_map.248 = (bf16[512,768]{1,0:T(8,128)(2,1)}, bf16[512,768]{1,0:T(8,128)(2,1)}, bf16[640,256]{1,0:T(8,128)(2,1)}, f32[16,512]{1,0:T(8,128)}, f32[16,128]{1,0:T(8,128)}) custom-call(bf16[512,768]{1,0:T(8,128)(2,1)} %bitcast.13, bf16[512,768]{1,0:T(8,128)(2,1)} %bitcast.14, f32[768]{0:T(1024)} %g1_ref.1, f32[768]{0:T(1024)} %g2_ref.1, ...), custom_call_target="tpu_custom_call" | custom-call | tf_op jit(solution)/shard_map/pallas_call | solution.py:695
  114.1 4.4 %shard_map.249 = (bf16[512,768]{1,0:T(8,128)(2,1)}, bf16[512,768]{1,0:T(8,128)(2,1)}, f32[3,192]{1,0:T(4,128)}, f32[3,192]{1,0:T(4,128)}, f32[3,192]{1,0:T(4,128...) custom-call(bf16[512,768]{1,0:T(8,128)(2,1)} %get-tuple-element.27.o, ...), custom_call_target="tpu_custom_call" | custom-call | tf_op jit(solution)/shard_map/pallas_call | solution.py:727

commit v4 on v3

--- a/solution.py
+++ b/solution.py
@@ -68,26 +68,33 @@
     )
 
 
-def seq_peer(k, me):
-    g, t = k // 8, k % 8
-    dx, dc = 1 - g // 2, ((g + 1) // 2) % 2
-    dz = 4 + (1 - 2 * (t % 2)) * ((t + 1) // 2)
-    xh, z, c = me // 16, (me // 2) % 8, me % 2
-    return ((xh + dx) % 2) * 16 + ((z + dz) % 8) * 2 + (c + dc) % 2
+def each_seq_peer(me, act):
+    xh, z, c = me // 16, lax.rem(me // 2, 8), lax.rem(me, 2)
+    corners = [(1 - xh) * 16 + c, (1 - xh) * 16 + 1 - c, xh * 16 + 1 - c, xh * 16 + c]
+
+    def step(t, carry):
+        dz = 4 + (1 - 2 * lax.rem(t, 2)) * ((t + 1) // 2)
+        there = lax.rem(z + dz, 8) * 2
+        for corner in corners:
+            act(corner + there)
+        return carry
+
+    lax.fori_loop(0, 7, step, 0)
+    for corner in corners[:3]:
+        act(corner + z * 2)
 
 
 def greet(me_s, me_d):
     barrier = pltpu.get_barrier_semaphore()
 
-    def over_seq(k, carry):
-        pl.semaphore_signal(barrier, inc=1, device_id={"seq": seq_peer(k, me_s)}, device_id_type=MESH)
-        return carry
+    def over_seq(peer):
+        pl.semaphore_signal(barrier, inc=1, device_id={"seq": peer}, device_id_type=MESH)
 
     def over_dp(k, carry):
         pl.semaphore_signal(barrier, inc=1, device_id={"dp": lax.rem(me_d + k, ND)}, device_id_type=MESH)
         return carry
 
-    lax.fori_loop(0, NS - 1, over_seq, 0)
+    each_seq_peer(me_s, over_seq)
     lax.fori_loop(1, ND, over_dp, 0)
     return lambda: pl.semaphore_wait(barrier, NS - 1 + ND - 1)
 
@@ -101,12 +108,10 @@
         return ref.at[index] if self.lanes is None else ref.at[index, :, self.lanes]
 
     def start(self):
-        def send(k, carry):
-            peer = seq_peer(k, self.me)
+        def send(peer):
             remote(self.at(self.sbuf, peer), self.at(self.rbuf, self.me), *self.sems, {"seq": peer}).start()
-            return carry
-
-        lax.fori_loop(0, NS - 1, send, 0)
+
+        each_seq_peer(self.me, send)
         if self.lanes is None:
             self.rbuf[self.me] = self.sbuf[self.me]
         else:
@@ -395,7 +400,7 @@
             mf = m.astype(F32)
             n2[rows_of(rows), :] = (mf * factor_of(mf) * g2).astype(BF16)
 
-        tiles(HALF, 32, norm_second)
+        tiles(HALF, 64, norm_second)
         for n in range(NB):
             hbuf[...] = dot(n2[half, blk(n)], up_ref[:, blk(n, HB)])
 
@@ -407,7 +412,7 @@
                     act[rows_of(rows), wide] = value.astype(BF16)
                     dpre[rows_of(rows), wide] = (slope * dact[ii, n, rows, lanes]).astype(BF16)
 
-            tiles(HALF, 32, gelu)
+            tiles(HALF, 64, gelu)
             t768[:, blk(n)] = dot(dpre[half, blk(n, HB)], up_ref[:, blk(n, HB)], 1, 1)
 
         def norm_back_second(rows, t):
@@ -419,7 +424,7 @@
             d = cot_ref[rows_of(rows), :].astype(F32) + f2 * (s - u2 * jnp.mean(s * u2, axis=-1, keepdims=True))
             dmid[rows_of(rows), :] = d.astype(BF16)
 
-        tiles(HALF, 32, norm_back_second)
+        tiles(HALF, 64, norm_back_second)
         for n in range(NB):
             t768[:, blk(n)] = dot(dmid[half, blk(n)], ow_ref[:, blk(n)], 1, 1)
 

time: 119 us -> 114 us (0.958)
  Pallas kernels: 118 us -> 113 us
    pallas_call x1, Pallas kernels: 113 us -> 109 us  [body(): pl.pallas_call(main_kernel, out_shape=[shape((ROWS, D), BF16), shape((ROW...]
where the time goes in v4:
time: 114 us
  Pallas kernels  113 us (99%)
    pallas_call x1, Pallas kernels, body(): pl.pallas_call(main_kernel, out_shape=[shape((ROWS, D), BF16), shape((ROW...  109 us
    pallas_call x1, Pallas kernels, body(): pl.pallas_call(finish_kernel, out_shape=[shape((ROWS, D), BF16), shape((R...  4.38 us

profile of v4, /device:TPU:1, one launch (start us, length us, event | category | flops | bytes accessed | tf_op | source)
XLA Modules:
  0.0 114.0 jit_solution(8744460303163039732)
XLA Ops:
  0.6 108.8 %shard_map.248 = (bf16[512,768]{1,0:T(8,128)(2,1)}, bf16[512,768]{1,0:T(8,128)(2,1)}, bf16[640,256]{1,0:T(8,128)(2,1)}, f32[16,512]{1,0:T(8,128)}, f32[16,128]{1,0:T(8,128)}) custom-call(bf16[512,768]{1,0:T(8,128)(2,1)} %bitcast.13, bf16[512,768]{1,0:T(8,128)(2,1)} %bitcast.14, f32[768]{0:T(1024)} %g1_ref.1, f32[768]{0:T(1024)} %g2_ref.1, ...), custom_call_target="tpu_custom_call" | custom-call | tf_op jit(solution)/shard_map/pallas_call | solution.py:700
  109.4 4.4 %shard_map.249 = (bf16[512,768]{1,0:T(8,128)(2,1)}, bf16[512,768]{1,0:T(8,128)(2,1)}, f32[3,192]{1,0:T(4,128)}, f32[3,192]{1,0:T(4,128)}, f32[3,192]{1,0:T(4,128...) custom-call(bf16[512,768]{1,0:T(8,128)(2,1)} %get-tuple-element.27.o, ...), custom_call_target="tpu_custom_call" | custom-call | tf_op jit(solution)/shard_map/pallas_call | solution.py:732
